TPU v7x, 32 devices: a whole 2x2x4 slice. The times are simulated.
32 devices in a mesh: dp: 4 (over z), ctx: 8 (over y, x, core).
Axes of the slice: x: 2, y: 2, z: 4, core: 2. Of those that a mesh axis runs over, the one named last changes fastest.
Arguments:
- inputs: bfloat16 [4, 1024, 3072], P('dp', 'ctx'), may hold values from -0.125 to 0.125
- queries: bfloat16 [4, 1024, 4096], P('dp', 'ctx'), may hold values from -0.875 to 0.875
- keys: bfloat16 [4, 1024, 4096], P('dp', 'ctx'), may hold values from -0.875 to 0.875
- values: bfloat16 [4, 1024, 4096], P('dp', 'ctx'), may hold values from -0.875 to 0.875
- out_grad: bfloat16 [4, 1024, 4096], P('dp', 'ctx'), may hold values from -0.875 to 0.875
- log_gate: float32 [4, 32, 1024], P('dp', None, 'ctx'), may hold values from -1 to 0
- boundaries: int32 [4, 4], P('dp'), may hold values from 1 to 1023, as said below
Outputs:
- query_grad: bfloat16 [4, 1024, 4096], P('dp', 'ctx')
- key_grad: bfloat16 [4, 1024, 4096], P('dp', 'ctx')
- value_weight_grad: float32 [3072, 4096], P('ctx', 'dp')
Inputs may be any that keep to these rules, and one draw needn't show every extreme that they name: `boundaries`: boundary j of a sequence (counting from 0) lies between j * 256 + 1 and j * 256 + 255.
All inputs are finite; a program needn't handle non-finite values.
Results may differ from a plain program's by a relative error of at most 0.034.
Values may be sent and summed in bfloat16 or wider, within the bound.
A program may use at most 192 MiB of HBM per device.

v0:
```python
import jax
import jax.numpy as jnp
from jax import lax
from jax.sharding import PartitionSpec as P


def prefix(value, axis, join, neutral, backward):
    count, mine = (lax.axis_size(axis), lax.axis_index(axis))
    pieces = jax.tree.map(lambda part: lax.all_gather(part, axis), value)
    if backward:
        pieces = jax.tree.map(lambda part: part[::-1], pieces)
        mine = count - 1 - mine
    subtotal = jax.tree.map(
        lambda part, zero: jnp.full_like(part, 0) + jnp.asarray(zero, part.dtype), value, neutral
    )

    def turn(position, subtotal):
        longer = join(subtotal, jax.tree.map(lambda part: part[position], pieces))
        return jax.tree.map(lambda new, old: jnp.where(position < mine, new, old), longer, subtotal)

    return lax.fori_loop(0, count - 1, turn, subtotal)


def join_states(earlier, latter):
    decay_multiplier = earlier[0].astype(jnp.float32) * latter[0].astype(jnp.float32)
    state = latter[0].astype(jnp.float32)[:, None, None] * earlier[1].astype(jnp.float32) + latter[
        1
    ].astype(jnp.float32)
    return (decay_multiplier.astype(jnp.bfloat16), state.astype(jnp.bfloat16))


def head_major(array, tok_rows, head_count, head_size):
    return array[0].reshape(tok_rows, head_count, head_size).transpose(1, 0, 2)


def row_major(array, tok_rows, feature_width):
    return array.astype(jnp.bfloat16).transpose(1, 0, 2).reshape(tok_rows, feature_width)


def per_device(inputs, queries, keys, values, out_grad, log_gate, boundaries):
    tok_rows = queries.shape[1]
    feature_width = queries.shape[2]
    head_count = log_gate.shape[1]
    head_size = feature_width // head_count
    query_one = head_major(queries, tok_rows, head_count, head_size)
    key_one = head_major(keys, tok_rows, head_count, head_size)
    value_one = head_major(values, tok_rows, head_count, head_size)
    grad_one = head_major(out_grad, tok_rows, head_count, head_size)
    token_one = inputs[0]
    bounds = boundaries[0]
    begin_at = lax.axis_index("ctx") * tok_rows
    positions = begin_at + jnp.arange(tok_rows, dtype=jnp.int32)
    segment_ids = jnp.sum((bounds[None, :] <= positions[:, None]).astype(jnp.int32), axis=1)
    segment_in = jnp.sum((bounds <= begin_at - 1).astype(jnp.int32))
    cumulative = jnp.cumsum(log_gate[0], axis=1)
    enter_weight = jnp.where((segment_ids == segment_in)[None, :], jnp.exp(cumulative), 0.0)
    leave_weight = jnp.where(
        (segment_ids == segment_ids[-1])[None, :], jnp.exp(cumulative[:, -1:] - cumulative), 0.0
    )
    causal = (positions[:, None] >= positions[None, :]) & (
        segment_ids[:, None] == segment_ids[None, :]
    )
    decay_table = jnp.exp(
        jnp.where(causal[None], cumulative[:, :, None] - cumulative[:, None, :], -1e30)
    )
    through = enter_weight[:, -1].astype(jnp.bfloat16)
    weighted_keys = (leave_weight[:, :, None] * key_one).astype(jnp.bfloat16)
    local_state = jnp.einsum(
        "hsd,hse->hde", weighted_keys, value_one, preferred_element_type=jnp.float32
    )
    weighted_queries = (enter_weight[:, :, None] * query_one).astype(jnp.bfloat16)
    back_state = jnp.einsum(
        "htd,hte->hde", weighted_queries, grad_one, preferred_element_type=jnp.float32
    )
    neutral = (
        jnp.ones((head_count,), jnp.bfloat16),
        jnp.zeros((head_count, head_size, head_size), jnp.bfloat16),
    )
    carried_in = prefix(
        (through, local_state.astype(jnp.bfloat16)), "ctx", join_states, neutral, False
    )[1]
    carried_back = prefix(
        (through, back_state.astype(jnp.bfloat16)), "ctx", join_states, neutral, True
    )[1]
    score_grad = (
        decay_table
        * jnp.einsum("htd,hsd->hts", grad_one, value_one, preferred_element_type=jnp.float32)
    ).astype(jnp.bfloat16)
    score_keys = (
        decay_table
        * jnp.einsum("htd,hsd->hts", query_one, key_one, preferred_element_type=jnp.float32)
    ).astype(jnp.bfloat16)
    query_new = jnp.einsum(
        "hts,hsd->htd", score_grad, key_one, preferred_element_type=jnp.float32
    ) + enter_weight[:, :, None] * jnp.einsum(
        "hte,hde->htd", grad_one, carried_in, preferred_element_type=jnp.float32
    )
    key_new = jnp.einsum(
        "hts,htd->hsd", score_grad, query_one, preferred_element_type=jnp.float32
    ) + leave_weight[:, :, None] * jnp.einsum(
        "hse,hde->hsd", value_one, carried_back, preferred_element_type=jnp.float32
    )
    value_new = jnp.einsum(
        "hts,htd->hsd", score_keys, grad_one, preferred_element_type=jnp.float32
    ) + leave_weight[:, :, None] * jnp.einsum(
        "hsd,hde->hse", key_one, carried_back, preferred_element_type=jnp.float32
    )
    query_grad = row_major(query_new, tok_rows, feature_width).reshape(1, tok_rows, feature_width)
    key_grad = row_major(key_new, tok_rows, feature_width).reshape(1, tok_rows, feature_width)
    value_grad = row_major(value_new, tok_rows, feature_width)
    partial_rows = lax.psum_scatter(
        lax.dot_general(
            token_one, value_grad, (((0,), (0,)), ((), ())), preferred_element_type=jnp.float32
        ).astype(jnp.bfloat16),
        "ctx",
        scatter_dimension=0,
        tiled=True,
    )
    weight_grad = lax.psum_scatter(partial_rows, "dp", scatter_dimension=1, tiled=True).astype(
        jnp.float32
    )
    return (query_grad, key_grad, weight_grad)


def solution(mesh):
    in_specs = (
        P("dp", "ctx", None),
        P("dp", "ctx", None),
        P("dp", "ctx", None),
        P("dp", "ctx", None),
        P("dp", "ctx", None),
        P("dp", None, "ctx"),
        P("dp", None),
    )
    out_specs = (P("dp", "ctx", None), P("dp", "ctx", None), P("ctx", "dp"))
    return jax.shard_map(
        per_device, mesh=mesh, in_specs=in_specs, out_specs=out_specs, check_vma=False
    )
```

profile of v0, /device:TPU:0, one launch (start us, length us, event | category | flops | bytes accessed | tf_op | source)
XLA Modules:
  0.0 436.8 jit_solution(2761133157954875375)
XLA Ops:
  12.6 2.0 copy.74
  16.0 2.7 convolution_convert_fusion
  20.5 15.3 %all-reduce = bf16[256]{0:T(256)(128)(2,1)S(1)} all-reduce(bf16[256]{0:T(256)(128)(2,1)S(1)} %dynamic-update-slice), channel_id=2, replica_groups=mesh['dp'=4,'ctx'=8] {'ctx'}, use_global_device_ids=true, to_apply=%add | all-reduce | flops 256 | bytes 1024
  36.0 2.4 copy.82
  38.5 37.6 %all-gather.8.cloned.1.call-done = bf16[256,128,128]{2,1,0:T(8,128)(2,1)} async-done(((bf16[32,128,128]{2,1,0:T(8,128)(2,1)}), bf16[256,128,128]{2,1,0:T(8,128)(2,1)}) %all-gather.8.cloned.1.call-update) | async-done | bytes 8388624 | tf_op jit(solution)/shard_map/all_gather | solution.py:9
  76.1 10.3 %rev.7 = bf16[8,32,128,128]{3,2,1,0:T(8,128)(2,1)} reverse(bf16[8,32,128,128]{3,2,1,0:T(8,128)(2,1)} %bitcast.124), dimensions={0} | reverse | bytes 16777216 | tf_op jit(solution)/shard_map/rev | solution.py:11
  86.4 13.4 %while.29 = (s32[]{:T(128)}, bf16[32,128,128]{2,1,0:T(8,128)(2,1)S(1)}, s32[]{:T(128)}, bf16[8,32]{1,0:T(8,128)(2,1)S(1)}, bf16[8,32,128,128]{3,2,1,0:T(8,128)(2,1)}, /*index=5*/s32[]{:T(128)}, s32[]{:T(128)}) while((s32[]{:T(128)}, bf16[32,128,128]{2,1,0:T(8,128)(2,1)S(1)}, s32[]{:T(128)}, bf16[8,32]{1,0:T(8,128)(2,1)S(1)}, ...), condition=%wide.region_6.7_spmd.clone, body=%wide.region_5.6_spmd.clone.sunk | while | flops 3670052 | bytes 3146161 | solution.py:21
  99.8 3.4 fusion.20
  103.3 4.7 %fusion.5 = bf16[128,32,128]{0,2,1:T(8,128)(2,1)} fusion(f32[32,128,128]{2,1,0:T(8,128)} %fusion.20, bf16[32,128,128]{1,2,0:T(8,128)(2,1)S(1)} %bitcast.114, f32[128,32]{0,1:T(8,128)S(1)} %bitcast.136, f32[32,128]{1,0:T(8,128)S(1)} %reduce_window_sum.11, pred[128,128]{1,0:T(8,128)(4,1)S(1)} %compare_and_fusion, bf16[128,32,128]{2,1,0:T(8,128)(2,1)} %bitcast.118, ...), kind=kOutput, calls=%fused_computation.11 | convolution fusion | flops 272105472 | bytes 6340608 | tf_op jit(solution)/shard_map/hts,htd->hsd/dot_general | solution.py:103
  108.0 13.1 %convert_bitcast_fusion = bf16[3072,4096]{0,1:T(8,128)(2,1)} fusion(bf16[128,4096]{0,1:T(8,128)(2,1)} %bitcast.131, bf16[1,128,3072]{2,1,0:T(8,128)(2,1)S(1)} %copy-done), kind=kOutput, calls=%fused_computation.8 | convolution fusion | flops 3233808384 | bytes 27000832 | tf_op jit(solution)/shard_map/dot_general | solution.py:112
  121.1 30.8 %copy.79 = bf16[3072,4096]{1,0:T(8,128)(2,1)} copy(bf16[3072,4096]{0,1:T(8,128)(2,1)} %convert_bitcast_fusion) | data formatting | bytes 50331648
  154.6 3.6 convolution_convert_fusion.1
  158.3 150.7 %reduce-scatter.7.cloned.1.call-done = bf16[384,4096]{1,0:T(8,128)(2,1)} async-done(((bf16[3072,4096]{1,0:T(8,128)(2,1)}), bf16[384,4096]{1,0:T(8,128)(2,1)}) %reduce-scatter.7.cloned.1.call-update) | async-done | bytes 3145744
  308.9 4.7 %copy.80 = bf16[384,4096]{0,1:T(8,128)(2,1)} copy(bf16[384,4096]{1,0:T(8,128)(2,1)} %reduce-scatter.7.cloned.1.call-done) | data formatting | bytes 6291456
  313.6 2.8 multiply_convert_fusion.3
  317.8 2.2 fusion.15
  321.9 2.3 copy.64
  324.1 41.1 %all-gather.6.cloned.1.call-done = bf16[256,128,128]{2,1,0:T(8,128)(2,1)} async-done(((bf16[32,128,128]{2,1,0:T(8,128)(2,1)}), bf16[256,128,128]{2,1,0:T(8,128)(2,1)}) %all-gather.6.cloned.1.call-update) | async-done | bytes 8388624 | tf_op jit(solution)/shard_map/all_gather | solution.py:9
  365.2 13.7 %while.28 = (s32[]{:T(128)}, bf16[32,128,128]{2,1,0:T(8,128)(2,1)S(1)}, s32[]{:T(128)}, bf16[8,32]{1,0:T(8,128)(2,1)S(1)}, bf16[8,32,128,128]{3,2,1,0:T(8,128)(2,1)}, /*index=5*/s32[]{:T(128)}, s32[]{:T(128)}) while((s32[]{:T(128)}, bf16[32,128,128]{2,1,0:T(8,128)(2,1)S(1)}, s32[]{:T(128)}, bf16[8,32]{1,0:T(8,128)(2,1)S(1)}, ...), condition=%wide.region_4.5_spmd.clone, body=%wide.region_3.4_spmd.clone.sunk | while | flops 3670052 | bytes 3146161 | solution.py:21
  373.0 2.1 fusion.57
  379.0 3.0 fusion.9
  382.0 2.3 copy.63
  384.3 43.3 %reduce-scatter.5.cloned.1.call-done = bf16[384,1024]{0,1:T(8,128)(2,1)} async-done(((bf16[384,4096]{0,1:T(8,128)(2,1)}), bf16[384,1024]{0,1:T(8,128)(2,1)}) %reduce-scatter.5.cloned.1.call-update) | async-done | bytes 786448 | tf_op jit(solution)/shard_map/reduce_scatter | solution.py:119
  427.7 2.5 copy.65
  (78 shorter events, 38.5 us)
Async XLA Ops:
  7.2 100.8 %copy-start = (bf16[1,128,3072]{2,1,0:T(8,128)(2,1)S(1)}, bf16[1,128,3072]{2,1,0:T(8,128)(2,1)}, u32[]{:S(2)}) copy-start(bf16[1,128,3072]{2,1,0:T(8,128)(2,1)} %param.11) | copy-start | bytes 2359300
  7.2 68.9 %all-gather.8.cloned.1.call-start = ((), (), s32[]{:S(2)}) async-start(), calls=%async_computation.4 | async-start | bytes 9437184 | tf_op jit(solution)/shard_map/all_gather | solution.py:9
  12.6 6.2 %copy-start.4 = (bf16[16,8,32,128]{3,2,1,0:T(8,128)(2,1)}, bf16[16,8,32,128]{3,2,1,0:T(8,128)(2,1)S(1)}, u32[]{:S(2)}) copy-start(bf16[16,8,32,128]{3,2,1,0:T(8,128)(2,1)S(1)} %copy.83) | copy-start | bytes 3145732
  14.6 88.7 %copy-start.2 = (bf16[1,128,4096]{1,2,0:T(8,128)(2,1)}, bf16[1,128,4096]{1,2,0:T(8,128)(2,1)S(1)}, u32[]{:S(2)}) copy-start(bf16[1,128,4096]{1,2,0:T(8,128)(2,1)S(1)} %copy.74) | copy-start | bytes 3145732
  16.0 2.8 copy-start.10
  18.8 290.2 %reduce-scatter.7.cloned.1.call-start = ((), (), s32[]{:S(2)}) async-start(), calls=%async_computation.5 | async-start | bytes 28311552
  151.9 2.8 copy-start.6
  151.9 213.3 %all-gather.6.cloned.1.call-start = ((), (), s32[]{:S(2)}) async-start(), calls=%async_computation.3 | async-start | bytes 9437184 | tf_op jit(solution)/shard_map/all_gather | solution.py:9
  153.7 1.0 copy-start.8
  158.2 269.4 %reduce-scatter.5.cloned.1.call-start = ((), (), s32[]{:S(2)}) async-start(), calls=%async_computation.2 | async-start | bytes 3932160 | tf_op jit(solution)/shard_map/reduce_scatter | solution.py:119
  313.6 2.9 copy-start.5
  316.5 1.3 copy-start.7
  317.8 2.2 copy-start.9
  365.2 13.7 %copy-start.3 = (bf16[1,128,4096]{1,2,0:T(8,128)(2,1)S(1)}, bf16[1,128,4096]{1,2,0:T(8,128)(2,1)}, u32[]{:S(2)}) copy-start(bf16[1,128,4096]{1,2,0:T(8,128)(2,1)} %copy-done.2) | copy-start | bytes 3145732
  382.0 48.2 %copy-start.1 = (bf16[1,128,3072]{2,1,0:T(8,128)(2,1)S(1)}, bf16[1,128,3072]{2,1,0:T(8,128)(2,1)}, u32[]{:S(2)}) copy-start(bf16[1,128,3072]{2,1,0:T(8,128)(2,1)} %param.11) | copy-start | bytes 2359300
Sparse Core Ops, SparseCore 0:
  18.9 57.1 all-gather.7
  152.0 156.8 reduce-scatter.6
  310.8 54.3 all-gather.5
  367.4 60.2 reduce-scatter.4
where the time goes:
time: 439 us; the launch traced here: 437 us
  waiting for transfers between devices  273 us (62%)
  local copies, waits for them, and re-layouts  64 us (15%)
  matrix products  38 us (9%)
  other arithmetic  31.2 us (7%)
  blocking collectives  15.3 us (3%)
  between operations  14.6 us (3%)
    unnamed x5, waiting for transfers between devices  151 us
    all_gather x2, waiting for transfers between devices, prefix(): pieces = jax.tree.map(lambda part: lax.all_gather(part, axis), value)  78.7 us
    unnamed x33, local copies, waits for them, and re-layouts  50.6 us
    reduce_scatter x1, waiting for transfers between devices, per_device(): lax.psum_scatter(partial_rows, 'dp', scatter_dimension=1, tiled=True)  43.3 us
    select_n x14, other arithmetic, turn(): jnp.where(position < mine, new, old)  26.5 us
    unnamed x1, blocking collectives  15.3 us
    dot_general x1, matrix products, per_device(): lax.dot_general(token_one, value_grad, (((0,), (0,)), ((), ())), preferre...  13.1 us
    rev x2, local copies, waits for them, and re-layouts, prefix(): pieces = jax.tree.map(lambda part: part[::-1], pieces)  10.4 us
  transfers between devices with their start and end apart: 4, of which 4 were waited for; matrix products, arithmetic and copies ran while one was open for 10% of the time, Pallas kernels for 0%

commit v1 on v0

--- a/solution.py
+++ b/solution.py
@@ -2,31 +2,6 @@
 import jax.numpy as jnp
 from jax import lax
 from jax.sharding import PartitionSpec as P
-
-
-def prefix(value, axis, join, neutral, backward):
-    count, mine = (lax.axis_size(axis), lax.axis_index(axis))
-    pieces = jax.tree.map(lambda part: lax.all_gather(part, axis), value)
-    if backward:
-        pieces = jax.tree.map(lambda part: part[::-1], pieces)
-        mine = count - 1 - mine
-    subtotal = jax.tree.map(
-        lambda part, zero: jnp.full_like(part, 0) + jnp.asarray(zero, part.dtype), value, neutral
-    )
-
-    def turn(position, subtotal):
-        longer = join(subtotal, jax.tree.map(lambda part: part[position], pieces))
-        return jax.tree.map(lambda new, old: jnp.where(position < mine, new, old), longer, subtotal)
-
-    return lax.fori_loop(0, count - 1, turn, subtotal)
-
-
-def join_states(earlier, latter):
-    decay_multiplier = earlier[0].astype(jnp.float32) * latter[0].astype(jnp.float32)
-    state = latter[0].astype(jnp.float32)[:, None, None] * earlier[1].astype(jnp.float32) + latter[
-        1
-    ].astype(jnp.float32)
-    return (decay_multiplier.astype(jnp.bfloat16), state.astype(jnp.bfloat16))
 
 
 def head_major(array, tok_rows, head_count, head_size):
@@ -72,16 +47,26 @@
     back_state = jnp.einsum(
         "htd,hte->hde", weighted_queries, grad_one, preferred_element_type=jnp.float32
     )
-    neutral = (
-        jnp.ones((head_count,), jnp.bfloat16),
-        jnp.zeros((head_count, head_size, head_size), jnp.bfloat16),
+    groups = lax.axis_size("ctx")
+    extra = jnp.broadcast_to(through[:, None, None], (head_count, 16, head_size))
+    packed = jnp.concatenate(
+        [local_state.astype(jnp.bfloat16), back_state.astype(jnp.bfloat16), extra], axis=1
     )
-    carried_in = prefix(
-        (through, local_state.astype(jnp.bfloat16)), "ctx", join_states, neutral, False
-    )[1]
-    carried_back = prefix(
-        (through, back_state.astype(jnp.bfloat16)), "ctx", join_states, neutral, True
-    )[1]
+    packed = lax.all_to_all(packed, "ctx", 0, 0, tiled=True)
+    packed = packed.reshape(groups, head_count // groups, 2 * head_size + 16, head_size)
+    ahead = packed[:, :, :head_size].astype(jnp.float32)
+    behind = packed[:, :, head_size : 2 * head_size].astype(jnp.float32)
+    factor = packed[:, :, 2 * head_size, :1, None].astype(jnp.float32)
+    state_in = [jnp.zeros_like(ahead[0])]
+    state_back = [jnp.zeros_like(ahead[0])]
+    for block in range(groups - 1):
+        state_in.append(factor[block] * state_in[-1] + ahead[block])
+        late = groups - 1 - block
+        state_back.append(factor[late] * state_back[-1] + behind[late])
+    carried = jnp.concatenate([jnp.stack(state_in), jnp.stack(state_back[::-1])], axis=2)
+    carried = carried.astype(jnp.bfloat16).reshape(head_count, 2 * head_size, head_size)
+    carried = lax.all_to_all(carried, "ctx", 0, 0, tiled=True)
+    carried_in, carried_back = carried[:, :head_size], carried[:, head_size:]
     score_grad = (
         decay_table
         * jnp.einsum("htd,hsd->hts", grad_one, value_one, preferred_element_type=jnp.float32)
@@ -108,16 +93,16 @@
     query_grad = row_major(query_new, tok_rows, feature_width).reshape(1, tok_rows, feature_width)
     key_grad = row_major(key_new, tok_rows, feature_width).reshape(1, tok_rows, feature_width)
     value_grad = row_major(value_new, tok_rows, feature_width)
-    partial_rows = lax.psum_scatter(
-        lax.dot_general(
-            token_one, value_grad, (((0,), (0,)), ((), ())), preferred_element_type=jnp.float32
-        ).astype(jnp.bfloat16),
-        "ctx",
-        scatter_dimension=0,
-        tiled=True,
-    )
-    weight_grad = lax.psum_scatter(partial_rows, "dp", scatter_dimension=1, tiled=True).astype(
-        jnp.float32
+    token_all = lax.all_to_all(token_one, "ctx", 1, 0, tiled=True)
+    token_all = lax.all_gather(token_all, "dp")
+    value_all = lax.all_to_all(value_grad, "dp", 1, 0, tiled=True)
+    value_all = lax.all_gather(value_all, "ctx")
+    sequences = token_all.shape[0]
+    token_all = token_all.reshape(sequences, groups, tok_rows, -1).transpose(1, 0, 2, 3)
+    token_all = token_all.reshape(groups * sequences * tok_rows, -1)
+    value_all = value_all.reshape(groups * sequences * tok_rows, -1)
+    weight_grad = lax.dot_general(
+        token_all, value_all, (((0,), (0,)), ((), ())), preferred_element_type=jnp.float32
     )
     return (query_grad, key_grad, weight_grad)
 

time: 439 us -> 215 us (0.49)
  waiting for transfers between devices: 273 us -> 88.7 us
  local copies, waits for them, and re-layouts: 64 us -> 24.4 us
  other arithmetic: 31.2 us -> 14 us
  blocking collectives: 15.3 us -> 28.4 us
  starting transfers between devices: 0.34 us -> 13.3 us
  matrix products: 38 us -> 31.3 us
    unnamed x5 -> x2, waiting for transfers between devices: 151 us -> 0.03 us
    all_to_all x0 -> x3, waiting for transfers between devices: none -> 51.4 us  [the longest x1 26.4 us: per_device(): carried = lax.all_to_all(carried, 'ctx', 0, 0, tiled=True)]
    reduce_scatter x1 -> x0, waiting for transfers between devices: 43.3 us -> none  [per_device(): lax.psum_scatter(partial_rows, 'dp', scatter_dimension=1, tiled=True)]
    all_gather x2, waiting for transfers between devices: 78.7 us -> 37.2 us  [the longest x1 37.2 us: per_device(): value_all = lax.all_gather(value_all, 'ctx')]
    unnamed x33 -> x38, local copies, waits for them, and re-layouts: 50.6 us -> 14.9 us
    all_to_all x0 -> x1, blocking collectives: none -> 28.4 us  [per_device(): value_all = lax.all_to_all(value_grad, 'dp', 1, 0, tiled=True)]
    select_n x14 -> x0, other arithmetic: 26.5 us -> none  [turn(): jnp.where(position < mine, new, old)]
    unnamed x1 -> x0, blocking collectives: 15.3 us -> none
  transfers between devices with their start and end apart: 4 -> 5, of which waited for: 4 -> 3; matrix products, arithmetic and copies ran while one was open for 10% -> 25% of each run, Pallas kernels for 0% -> 0%
where the time goes in v1:
time: 215 us; the launch traced here: 214 us
  waiting for transfers between devices  88.7 us (41%)
  matrix products  31.3 us (15%)
  blocking collectives  28.4 us (13%)
  local copies, waits for them, and re-layouts  24.4 us (11%)
  between operations  14.3 us (7%)
  other arithmetic  14 us (7%)
  starting transfers between devices  13.3 us (6%)
    all_gather x1, waiting for transfers between devices, per_device(): value_all = lax.all_gather(value_all, 'ctx')  37.2 us
    all_to_all x1, blocking collectives, per_device(): value_all = lax.all_to_all(value_grad, 'dp', 1, 0, tiled=True)  28.4 us
    all_to_all x1, waiting for transfers between devices, per_device(): carried = lax.all_to_all(carried, 'ctx', 0, 0, tiled=True)  26.4 us
    all_to_all x1, waiting for transfers between devices, per_device(): packed = lax.all_to_all(packed, 'ctx', 0, 0, tiled=True)  25 us
    unnamed x38, local copies, waits for them, and re-layouts  14.9 us
    dot_general x1, matrix products, per_device(): lax.dot_general(token_all, value_all, (((0,), (0,)), ((), ())), preferred...  8.15 us
    all_to_all x1, starting transfers between devices, per_device(): token_all = lax.all_to_all(token_one, 'ctx', 1, 0, tiled=True)  5.3 us
    unnamed x11, other arithmetic  5.1 us
  transfers between devices with their start and end apart: 5, of which 3 were waited for; matrix products, arithmetic and copies ran while one was open for 25% of the time, Pallas kernels for 0%

profile of v1, /device:TPU:0, one launch (start us, length us, event | category | flops | bytes accessed | tf_op | source)
XLA Modules:
  0.0 214.4 jit_solution(13207365834612911095)
XLA Ops:
  7.2 2.4 %copy.113 = bf16[1,128,3072]{1,2,0:T(8,128)(2,1)} copy(bf16[1,128,3072]{2,1,0:T(8,128)(2,1)} %param.7) | data formatting | bytes 1572864 | tf_op args[0]
  9.6 5.3 %all-to-all-start.3 = ((bf16[128,8,384]{0,2,1:T(8,128)(2,1)}), bf16[128,8,384]{0,2,1:T(8,128)(2,1)}, u32[]{:S(2)}, u32[]{:S(2)}) async-start(bf16[128,8,384]{0,2,1:T(8,128)(2,1)} %bitcast.36), calls=%async_computation.3 | async-start | bytes 1572864 | tf_op jit(solution)/shard_map/all_to_all | solution.py:96
  21.7 1.9 convolution_convert_fusion
  23.7 2.8 %convolution_convert_fusion.1 = bf16[32,128,128]{2,1,0:T(8,128)(2,1)S(1)} fusion(f32[32,128]{1,0:T(8,128)S(1)} %get-tuple-element.33, bf16[128,32,128]{2,1,0:T(8,128)(2,1)S(1)} %bitcast.122, bf16[128,32,128]{2,1,0:T(8,128)(2,1)S(1)} %bitcast.128), kind=kOutput, calls=%fused_computation.18 | convolution fusion | flops 136314880 | bytes 3162112 | tf_op jit(solution)/shard_map/hsd,hse->hde/dot_general | solution.py:43
  28.1 4.4 %all-to-all-start = ((bf16[32,272,128]{2,1,0:T(8,128)(2,1)}), bf16[32,272,128]{2,1,0:T(8,128)(2,1)}, u32[]{:S(2)}, u32[]{:S(2)}) async-start(bf16[32,272,128]{2,1,0:T(8,128)(2,1)} %pad_maximum_fusion), calls=%async_computation | async-start | bytes 4456448 | tf_op jit(solution)/shard_map/all_to_all | solution.py:55
  33.2 2.3 %copy.114 = bf16[8,128,384]{2,1,0:T(8,128)(2,1)} copy(bf16[8,128,384]{1,2,0:T(8,128)(2,1)} %bitcast.37) | data formatting | bytes 1572864 | tf_op jit(solution)/shard_map/all_to_all | solution.py:96
  35.5 25.0 %all-to-all-done = bf16[32,272,128]{2,1,0:T(8,128)(2,1)} async-done(((bf16[32,272,128]{2,1,0:T(8,128)(2,1)}), bf16[32,272,128]{2,1,0:T(8,128)(2,1)}, u32[]{:S(2)}, u32[]{:S(2)}) %all-to-all-start) | async-done | bytes 2228256 | tf_op jit(solution)/shard_map/all_to_all | solution.py:55
  60.5 3.4 %slice_convert_fusion.1 = (f32[8,4,128,128]{3,2,1,0:T(8,128)S(1)}, f32[8,4,128,128]{3,2,1,0:T(8,128)}) fusion(bf16[8,4,272,128]{3,2,1,0:T(8,128)(2,1)} %bitcast.12), kind=kLoop, calls=%fused_computation.21 | loop fusion | flops 1048576 | bytes 6291456 | tf_op jit(solution)/shard_map/convert_element_type | solution.py:57
  71.0 1.6 pad_maximum_fusion.1
  72.6 3.6 %all-to-all-start.1 = ((bf16[32,256,128]{2,1,0:T(8,128)(2,1)}), bf16[32,256,128]{2,1,0:T(8,128)(2,1)S(1)}, u32[]{:S(2)}, u32[]{:S(2)}) async-start(bf16[32,256,128]{2,1,0:T(8,128)(2,1)} %pad_maximum_fusion.1), calls=%async_computation.1 | async-start | bytes 4194304 | tf_op jit(solution)/shard_map/all_to_all | solution.py:68
  76.3 26.4 %all-to-all-done.1 = bf16[32,256,128]{2,1,0:T(8,128)(2,1)S(1)} async-done(((bf16[32,256,128]{2,1,0:T(8,128)(2,1)}), bf16[32,256,128]{2,1,0:T(8,128)(2,1)S(1)}, u32[]{:S(2)}, u32[]{:S(2)}) %all-to-all-start.1) | async-done | bytes 2097184 | tf_op jit(solution)/shard_map/all_to_all | solution.py:68
  102.7 3.5 %fusion.17 = f32[32,128,128]{2,1,0:T(8,128)} fusion(bf16[32,256,128]{2,1,0:T(8,128)(2,1)S(1)} %all-to-all-done.1, bf16[128,32,128]{2,1,0:T(8,128)(2,1)} %bitcast.123), kind=kOutput, calls=%fused_computation.30 | convolution fusion | flops 134217728 | bytes 4194304 | tf_op jit(solution)/shard_map/hsd,hde->hse/dot_general | solution.py:90
  106.2 4.7 %fusion.1 = bf16[128,32,128]{0,2,1:T(8,128)(2,1)} fusion(f32[32,128,128]{2,1,0:T(8,128)} %fusion.17, bf16[32,128,128]{1,2,0:T(8,128)(2,1)S(1)} %bitcast.116, f32[128,32]{0,1:T(8,128)S(1)} %bitcast.142, f32[32,128]{1,0:T(8,128)S(1)} %reduce_window_sum.11, pred[128,128]{1,0:T(8,128)(4,1)S(1)} %compare_and_fusion, bf16[128,32,128]{2,1,0:T(8,128)(2,1)} %bitcast.120, ...), kind=kOutput, calls=%fused_computation.4 | convolution fusion | flops 272105472 | bytes 6340608 | tf_op jit(solution)/shard_map/hts,htd->hsd/dot_general | solution.py:88
  110.9 2.3 %copy.112 = bf16[128,4,1024]{2,0,1:T(8,128)(2,1)} copy(bf16[128,4,1024]{0,2,1:T(8,128)(2,1)} %bitcast.140) | data formatting | bytes 2097152 | tf_op jit(solution)/shard_map/all_to_all | solution.py:98
  113.2 28.4 %all_to_all.42 = bf16[128,4,1024]{2,0,1:T(8,128)(2,1)} all-to-all(bf16[128,4,1024]{2,0,1:T(8,128)(2,1)} %copy.112), channel_id=1, replica_groups=mesh['dp'=4,'ctx'=8] {'dp'}, dimensions={1} | all-to-all | bytes 2097152 | tf_op jit(solution)/shard_map/all_to_all | solution.py:98
  141.6 2.5 %multiply_convert_fusion.3 = bf16[32,128,128]{2,1,0:T(8,128)(2,1)S(1)} fusion(bf16[32,128,128]{1,2,0:T(8,128)(2,1)S(1)} %bitcast.117, f32[32,128]{1,0:T(8,128)S(1)} %reduce_window_sum.11, pred[128,128]{1,0:T(8,128)(4,1)S(1)} %compare_and_fusion, bf16[128,32,128]{2,1,0:T(8,128)(2,1)} %bitcast.127), kind=kOutput, calls=%fused_computation.14 | convolution fusion | flops 136314880 | bytes 3178496 | tf_op jit(solution)/shard_map/htd,hsd->hts/dot_general | solution.py:72
  145.4 2.0 fusion.7
  148.9 2.4 %copy.116 = bf16[1,128,4096]{2,1,0:T(8,128)(2,1)} copy(bf16[1,128,4096]{1,2,0:T(8,128)(2,1)} %bitcast.131) | data formatting | bytes 2097152
  151.3 3.4 %fusion.3 = bf16[128,32,128]{0,2,1:T(8,128)(2,1)} fusion(f32[32,128,128]{1,2,0:T(8,128)} %fusion.7, f32[128,32]{0,1:T(8,128)S(1)} %bitcast.143, bf16[32,256,128]{2,1,0:T(8,128)(2,1)S(1)} %all-to-all-done.1, bf16[128,32,128]{2,1,0:T(8,128)(2,1)S(1)} %bitcast.129), kind=kOutput, calls=%fused_computation.7 | convolution fusion | flops 135790592 | bytes 5259264 | tf_op jit(solution)/shard_map/hse,hde->hsd/dot_general | solution.py:85
  154.7 2.3 %copy.117 = bf16[1,128,4096]{2,1,0:T(8,128)(2,1)} copy(bf16[1,128,4096]{1,2,0:T(8,128)(2,1)} %bitcast.130) | data formatting | bytes 2097152
  156.9 2.2 %copy.115 = bf16[8,4,128,384]{3,2,1,0:T(8,128)(2,1)S(1)} copy(bf16[8,4,128,384]{3,2,0,1:T(8,128)(2,1)} %bitcast.133) | data formatting | bytes 6291456 | tf_op jit(solution)/shard_map/transpose | solution.py:101
  159.2 37.2 %all-gather.3.cloned.1.call-done = bf16[8,512,1024]{2,1,0:T(8,128)(2,1)} async-done(((bf16[1,512,1024]{2,1,0:T(8,128)(2,1)}), bf16[8,512,1024]{2,1,0:T(8,128)(2,1)}) %all-gather.3.cloned.1.call-update) | async-done | bytes 8388624 | tf_op jit(solution)/shard_map/all_gather | solution.py:99
  196.4 8.1 %convolution_bitcast_fusion = f32[384,1024]{0,1:T(8,128)} fusion(bf16[4096,1024]{1,0:T(8,128)(2,1)} %bitcast.126, bf16[4096,384]{1,0:T(8,128)(2,1)S(1)} %bitcast.114), kind=kOutput, calls=%fused_computation.16 | convolution fusion | flops 3221225472 | bytes 13107200 | tf_op jit(solution)/shard_map/dot_general | solution.py:104
  204.6 3.0 %copy.118 = f32[384,1024]{1,0:T(8,128)} copy(f32[384,1024]{0,1:T(8,128)} %convolution_bitcast_fusion) | data formatting | bytes 3145728
  (70 shorter events, 19.0 us)
Async XLA Ops:
  7.2 7.7 %copy-start.8 = (bf16[1,128,4096]{2,1,0:T(8,128)(2,1)S(1)}, bf16[1,128,4096]{2,1,0:T(8,128)(2,1)}, u32[]{:S(2)}) copy-start(bf16[1,128,4096]{2,1,0:T(8,128)(2,1)} %param.11) | copy-start | bytes 3145732
  9.5 6.0 %copy-start.9 = (bf16[1,128,4096]{2,1,0:T(8,128)(2,1)S(1)}, bf16[1,128,4096]{2,1,0:T(8,128)(2,1)}, u32[]{:S(2)}) copy-start(bf16[1,128,4096]{2,1,0:T(8,128)(2,1)} %param.10) | copy-start | bytes 3145732
  9.6 18.6 %all-to-all-start.3 = ((bf16[128,8,384]{0,2,1:T(8,128)(2,1)}), bf16[128,8,384]{0,2,1:T(8,128)(2,1)}, u32[]{:S(2)}, u32[]{:S(2)}) async-start(bf16[128,8,384]{0,2,1:T(8,128)(2,1)} %bitcast.36), calls=%async_computation.3 | async-start | bytes 1572864 | tf_op jit(solution)/shard_map/all_to_all | solution.py:96
  15.5 1.3 copy-start.10
  15.6 1.5 copy-start.12
  15.6 2.0 copy-start.13
  16.8 3.7 %copy-start.11 = (bf16[1,128,4096]{2,1,0:T(8,128)(2,1)S(1)}, bf16[1,128,4096]{2,1,0:T(8,128)(2,1)}, u32[]{:S(2)}) copy-start(bf16[1,128,4096]{2,1,0:T(8,128)(2,1)} %param.8) | copy-start | bytes 3145732
  17.1 11.1 %copy-start.3 = (bf16[16,8,32,128]{3,2,1,0:T(8,128)(2,1)}, bf16[16,8,32,128]{3,2,1,0:T(8,128)(2,1)S(1)}, u32[]{:S(2)}) copy-start(bf16[16,8,32,128]{3,2,1,0:T(8,128)(2,1)S(1)} %copy.134) | copy-start | bytes 3145732
  20.7 1.0 copy-start.1
  20.7 2.9 %copy-start.5 = (bf16[16,8,32,128]{3,2,1,0:T(8,128)(2,1)S(1)}, bf16[16,8,32,128]{3,2,1,0:T(8,128)(2,1)}, u32[]{:S(2)}) copy-start(bf16[16,8,32,128]{3,2,1,0:T(8,128)(2,1)} %copy.133) | copy-start | bytes 3145732
  28.1 32.4 %all-to-all-start = ((bf16[32,272,128]{2,1,0:T(8,128)(2,1)}), bf16[32,272,128]{2,1,0:T(8,128)(2,1)}, u32[]{:S(2)}, u32[]{:S(2)}) async-start(bf16[32,272,128]{2,1,0:T(8,128)(2,1)} %pad_maximum_fusion), calls=%async_computation | async-start | bytes 4456448 | tf_op jit(solution)/shard_map/all_to_all | solution.py:55
  32.5 124.5 %all-gather.5.cloned.1.call-start = ((), (), s32[]{:S(2)}) async-start(), calls=%async_computation.5 | async-start | bytes 3932160 | tf_op jit(solution)/shard_map/all_gather | solution.py:97
  64.9 3.8 %copy-start = (f32[8,4,128,128]{3,2,1,0:T(8,128)S(1)}, f32[8,4,128,128]{3,2,1,0:T(8,128)}, u32[]{:S(2)}) copy-start(f32[8,4,128,128]{3,2,1,0:T(8,128)} %get-tuple-element.32) | copy-start | bytes 6291460
  69.6 1.2 copy-start.7
  72.6 30.2 %all-to-all-start.1 = ((bf16[32,256,128]{2,1,0:T(8,128)(2,1)}), bf16[32,256,128]{2,1,0:T(8,128)(2,1)S(1)}, u32[]{:S(2)}, u32[]{:S(2)}) async-start(bf16[32,256,128]{2,1,0:T(8,128)(2,1)} %pad_maximum_fusion.1), calls=%async_computation.1 | async-start | bytes 4194304 | tf_op jit(solution)/shard_map/all_to_all | solution.py:68
  76.2 120.2 %all-gather.3.cloned.1.call-start = ((), (), s32[]{:S(2)}) async-start(), calls=%async_computation.4 | async-start | bytes 9437184 | tf_op jit(solution)/shard_map/all_gather | solution.py:99
  141.6 2.5 %copy-start.4 = (bf16[16,8,32,128]{3,2,1,0:T(8,128)(2,1)S(1)}, bf16[16,8,32,128]{3,2,1,0:T(8,128)(2,1)}, u32[]{:S(2)}) copy-start(bf16[16,8,32,128]{3,2,1,0:T(8,128)(2,1)} %copy-done.3) | copy-start | bytes 3145732
  144.2 1.2 copy-start.2
  148.9 2.4 %copy-start.6 = (bf16[16,8,32,128]{3,2,1,0:T(8,128)(2,1)S(1)}, bf16[16,8,32,128]{3,2,1,0:T(8,128)(2,1)}, u32[]{:S(2)}) copy-start(bf16[16,8,32,128]{3,2,1,0:T(8,128)(2,1)} %copy.133) | copy-start | bytes 3145732
Sparse Core Ops, SparseCore 0:
  35.7 65.5 all-gather.4
  141.7 54.6 all-gather.2

commit v2 on v1

--- a/solution.py
+++ b/solution.py
@@ -1,6 +1,10 @@
+import functools
+
 import jax
 import jax.numpy as jnp
 from jax import lax
+from jax.experimental import pallas as pl
+from jax.experimental.pallas import tpu as pltpu
 from jax.sharding import PartitionSpec as P
 
 
@@ -12,7 +16,7 @@
     return array.astype(jnp.bfloat16).transpose(1, 0, 2).reshape(tok_rows, feature_width)
 
 
-def per_device(inputs, queries, keys, values, out_grad, log_gate, boundaries):
+def per_device_plain(inputs, queries, keys, values, out_grad, log_gate, boundaries):
     tok_rows = queries.shape[1]
     feature_width = queries.shape[2]
     head_count = log_gate.shape[1]
@@ -107,6 +111,443 @@
     return (query_grad, key_grad, weight_grad)
 
 
+F32, BF16 = jnp.float32, jnp.bfloat16
+
+
+def dot(left, right, left_dim, right_dim):
+    return lax.dot_general(
+        left, right, (((left_dim,), (right_dim,)), ((), ())), preferred_element_type=F32
+    )
+
+
+def push(src, dst, send_sem, recv_sem, dp, ctx):
+    return pltpu.make_async_remote_copy(
+        src_ref=src,
+        dst_ref=dst,
+        send_sem=send_sem,
+        recv_sem=recv_sem,
+        device_id=(dp, ctx),
+        device_id_type=pl.DeviceIdType.MESH,
+    )
+
+
+def fused(
+    planes, blocks, q, k, v, g, x, gate, bounds, qg, kg, wg,
+    cum, decay_bias, enter_bias, leave_bias, through, xt_own, xt,
+    local, mate_local, chip_state, arrived, carried, mate_carried, qi, ki, vi, vsend, vall,
+    t_s, t_r, xa_s, xa_r, xz_s, xz_r, m1_s, m1_r, cs_s, cs_r, m2_s, m2_r, vz_s, vz_r,
+    vb_s, vb_r, vm_s, vm_r,
+):
+    tok, feature = q.shape
+    heads = gate.shape[0]
+    size = feature // heads
+    chunk = heads // planes
+    half = chunk // 2
+    rows = xt.shape[1]
+    chips = blocks // 2
+    d, c = lax.axis_index("dp"), lax.axis_index("ctx")
+    core, chip = lax.rem(c, 2), lax.div(c, 2)
+    mate = c + 1 - 2 * core
+    first = core == 0
+
+    barrier = pltpu.get_barrier_semaphore()
+    for step in range(1, blocks):
+        pl.semaphore_signal(
+            barrier, inc=1, device_id=(d, lax.rem(c + step, blocks)),
+            device_id_type=pl.DeviceIdType.MESH,
+        )
+    for step in range(1, planes):
+        pl.semaphore_signal(
+            barrier, inc=1, device_id=(lax.rem(d + step, planes), c),
+            device_id_type=pl.DeviceIdType.MESH,
+        )
+
+    for part in range(x.shape[1] // 128):
+        xt_own[part * 128 : (part + 1) * 128, :] = x[:, part * 128 : (part + 1) * 128].T
+    pl.semaphore_wait(barrier, blocks - 1 + planes - 1)
+
+    def columns(block):
+        return pl.ds(pl.multiple_of(block * tok, tok), tok)
+
+    def token_push(step):
+        to = lax.rem(c + step, blocks)
+        return push(
+            xt_own.at[pl.ds(pl.multiple_of(to * rows, rows), rows), :],
+            xt.at[d, :, columns(c)], xa_s.at[step - 1], xa_r.at[step - 1], d, to,
+        )
+
+    for step in range(1, blocks):
+        token_push(step).start()
+    xt[d, :, columns(c)] = xt_own[pl.ds(pl.multiple_of(c * rows, rows), rows), :]
+
+    begin = c * tok
+    at_t = lax.broadcasted_iota(jnp.int32, (tok, tok), 0)
+    at_s = lax.broadcasted_iota(jnp.int32, (tok, tok), 1)
+    seg_t = jnp.zeros((tok, tok), jnp.int32)
+    seg_s = jnp.zeros((tok, tok), jnp.int32)
+    seg_in = jnp.zeros((tok, tok), jnp.int32)
+    seg_last = jnp.zeros((tok, tok), jnp.int32)
+    for index in range(bounds.shape[1]):
+        edge = jnp.full((tok, tok), bounds[0, index] - begin, jnp.int32)
+        seg_t += (edge <= at_t).astype(jnp.int32)
+        seg_s += (edge <= at_s).astype(jnp.int32)
+        seg_in += (edge <= -1).astype(jnp.int32)
+        seg_last += (edge <= tok - 1).astype(jnp.int32)
+    decay_bias[...] = jnp.where((at_t >= at_s) & (seg_t == seg_s), 0.0, -1e30)
+    enter_bias[...] = jnp.where(seg_t == seg_in, 0.0, -1e30)
+    leave_bias[...] = jnp.where(seg_t == seg_last, 0.0, -1e30)
+    cum[...] = lax.dot_general(
+        gate[...], (at_t <= at_s).astype(F32), (((1,), (0,)), ((), ())),
+        precision=lax.Precision.HIGHEST, preferred_element_type=F32,
+    )
+    total = jnp.broadcast_to(cum[:, tok - 1 : tok], (heads, size))
+    through[c] = jnp.exp(total + enter_bias[tok - 1 : tok, :]).astype(BF16).astype(F32)
+
+    def through_push(step):
+        return push(
+            through.at[c], through.at[c], t_s.at[step - 1], t_r.at[step - 1],
+            d, lax.rem(c + step, blocks),
+        )
+
+    for step in range(1, blocks):
+        through_push(step).start()
+
+    def head_columns(head):
+        return pl.ds(pl.multiple_of(head * size, size), size)
+
+    def weights(head):
+        at_row = jnp.broadcast_to(cum[pl.ds(head, 1), :], (size, tok))
+        at_col = at_row.T
+        enter = jnp.exp(at_col + enter_bias[...])
+        leave = jnp.exp(at_col[tok - 1 : tok, :] - at_col + leave_bias[...])
+        return at_row, at_col, enter, leave
+
+    def chunk_head(i, j):
+        return lax.rem(d + i, planes) * chunk + j
+
+    def mate_push(i):
+        return push(local.at[i, 1 - core], mate_local.at[i], m1_s.at[i], m1_r.at[i], d, mate)
+
+    def local_chunk(i, carry):
+        for j in range(chunk):
+            head = chunk_head(i, j)
+            cols = head_columns(head)
+            _, _, enter, leave = weights(head)
+            weighted_keys = (leave * k[:, cols].astype(F32)).astype(BF16)
+            weighted_queries = (enter * q[:, cols].astype(F32)).astype(BF16)
+            local[i, j // half, 0, j % half] = dot(weighted_keys, v[:, cols], 0, 0).astype(BF16)
+            local[i, j // half, 1, j % half] = dot(weighted_queries, g[:, cols], 0, 0).astype(BF16)
+        mate_push(i).start()
+        return carry
+
+    lax.fori_loop(0, planes, local_chunk, 0)
+
+    for step in range(1, blocks):
+        frm = lax.rem(c - step + blocks, blocks)
+        push(
+            through.at[frm], through.at[frm], t_s.at[step - 1], t_r.at[step - 1], d, frm
+        ).wait_recv()
+
+    def state_push(i, step):
+        ahead = chip + step
+        return push(
+            chip_state.at[i, lax.div(ahead, chips)], arrived.at[i, step - 1],
+            cs_s.at[i, step - 1], cs_r.at[i, step - 1], d, 2 * lax.rem(ahead, chips) + core,
+        )
+
+    def chip_chunk(i, carry):
+        mate_push(i).wait_recv()
+        for j in range(half):
+            head = chunk_head(i, core * half + j)
+            mine = through[c, pl.ds(head, 1), :]
+            other = through[mate, pl.ds(head, 1), :]
+            chip_state[i, 0, j] = (
+                jnp.where(first, other, 1.0) * local[i, core, 0, j].astype(F32)
+                + jnp.where(first, 1.0, mine) * mate_local[i, 0, j].astype(F32)
+            ).astype(BF16)
+            chip_state[i, 1, j] = (
+                jnp.where(first, 1.0, other) * local[i, core, 1, j].astype(F32)
+                + jnp.where(first, mine, 1.0) * mate_local[i, 1, j].astype(F32)
+            ).astype(BF16)
+        for step in range(1, chips):
+            state_push(i, step).start()
+        return carry
+
+    lax.fori_loop(0, planes, chip_chunk, 0)
+
+    for step in range(1, blocks):
+        token_push(step).wait_send()
+        frm = lax.rem(c - step + blocks, blocks)
+        push(
+            xt.at[d, :, columns(frm)], xt.at[d, :, columns(frm)],
+            xa_s.at[step - 1], xa_r.at[step - 1], d, frm,
+        ).wait_recv()
+
+    def chain(step, act):
+        @pl.when((d >= step - 1) & (d + 1 < planes))
+        def _():
+            piece = xt.at[d - (step - 1)]
+            act(push(piece, piece, xz_s.at[0, step - 1], xz_r.at[0, step - 1], d + 1, c))
+
+        @pl.when((d + step - 1 < planes) & (d >= 1))
+        def _():
+            piece = xt.at[d + step - 1]
+            act(push(piece, piece, xz_s.at[1, step - 1], xz_r.at[1, step - 1], d - 1, c))
+
+    def chain_wait(step):
+        @pl.when(d >= step)
+        def _():
+            piece = xt.at[d - step]
+            push(piece, piece, xz_s.at[0, step - 1], xz_r.at[0, step - 1], d - 1, c).wait_recv()
+
+        @pl.when(d + step < planes)
+        def _():
+            piece = xt.at[d + step]
+            push(piece, piece, xz_s.at[1, step - 1], xz_r.at[1, step - 1], d + 1, c).wait_recv()
+
+    chain(1, lambda copy: copy.start())
+
+    group = 4
+
+    def inner(index, carry):
+        for j in range(group):
+            head = index * group + j
+            cols = head_columns(head)
+            at_row = jnp.broadcast_to(cum[pl.ds(head, 1), :], (size, tok))
+            decay = jnp.exp(at_row.T - at_row + decay_bias[...])
+            qh, kh, vh, gh = q[:, cols], k[:, cols], v[:, cols], g[:, cols]
+            score_grad = (decay * dot(gh, vh, 1, 1)).astype(BF16)
+            score_keys = (decay * dot(qh, kh, 1, 1)).astype(BF16)
+            qi[:, cols] = dot(score_grad, kh, 1, 0)
+            ki[:, cols] = dot(score_grad, qh, 0, 0)
+            vi[:, cols] = dot(score_keys, gh, 0, 0)
+        return carry
+
+    lax.fori_loop(0, heads // group, inner, 0)
+
+    def carried_push(i):
+        return push(mate_carried.at[i], carried.at[i, core], m2_s.at[i], m2_r.at[i], d, mate)
+
+    def carry_chunk(i):
+        for step in range(1, chips):
+            state_push(i, step).wait_recv()
+        for j in range(half):
+            head = chunk_head(i, core * half + j)
+            mine = through[c, pl.ds(head, 1), :]
+            other = through[mate, pl.ds(head, 1), :]
+            sums = []
+            for back in (False, True):
+                state = jnp.zeros((size, size), F32)
+                weight = jnp.ones((1, size), F32)
+                for far in range(1, chips):
+                    if back:
+                        valid = chip + far < chips
+                        source, slot = lax.rem(chip + far, chips), chips - far - 1
+                    else:
+                        valid = chip >= far
+                        source, slot = lax.rem(chip - far + chips, chips), far - 1
+                    state += jnp.where(valid, weight, 0.0) * arrived[i, slot, j].astype(F32)
+                    weight = weight * (
+                        through[2 * source, pl.ds(head, 1), :]
+                        * through[2 * source + 1, pl.ds(head, 1), :]
+                    )
+                sums.append(state)
+            came, back = sums
+            late = jnp.where(first, 0.0, 1.0)
+            early = 1.0 - late
+            carried[i, core, 0, j] = (
+                jnp.where(first, 1.0, other) * came + late * mate_local[i, 0, j].astype(F32)
+            ).astype(BF16)
+            carried[i, core, 1, j] = (
+                jnp.where(first, other, 1.0) * back + early * mate_local[i, 1, j].astype(F32)
+            ).astype(BF16)
+            mate_carried[i, 0, j] = (
+                jnp.where(first, mine, 1.0) * came + early * local[i, core, 0, j].astype(F32)
+            ).astype(BF16)
+            mate_carried[i, 1, j] = (
+                jnp.where(first, 1.0, mine) * back + late * local[i, core, 1, j].astype(F32)
+            ).astype(BF16)
+        carried_push(i).start()
+
+    def value_push(i):
+        return push(
+            vsend.at[i], vall.at[d, c], vz_s.at[i], vz_r.at[i], lax.rem(d + i, planes), c
+        )
+
+    def finish(i):
+        push(
+            carried.at[i, 1 - core], carried.at[i, 1 - core], m2_s.at[i], m2_r.at[i], d, mate
+        ).wait_recv()
+        for j in range(chunk):
+            head = chunk_head(i, j)
+            cols = head_columns(head)
+            _, _, enter, leave = weights(head)
+            came = carried[i, j // half, 0, j % half]
+            back = carried[i, j // half, 1, j % half]
+            vsend[i, :, j * size : (j + 1) * size] = (
+                vi[:, cols] + leave * dot(k[:, cols], back, 1, 0)
+            ).astype(BF16)
+            qg[:, cols] = (qi[:, cols] + enter * dot(g[:, cols], came, 1, 1)).astype(BF16)
+            kg[:, cols] = (ki[:, cols] + leave * dot(v[:, cols], back, 1, 1)).astype(BF16)
+        if i == 0:
+            vall[d, c] = vsend[0]
+        else:
+            value_push(i).start()
+
+    def source_plane(i):
+        return lax.rem(d - i + planes, planes)
+
+    def spread(i, act):
+        piece = vall.at[source_plane(i), c]
+        for step in range(1, chips):
+            to = 2 * lax.rem(chip + step, chips) + core
+            act(push(piece, piece, vb_s.at[i, step - 1], vb_r.at[i, step - 1], d, to))
+        act(push(piece, piece, vm_s.at[i, 0], vm_r.at[i, 0], d, mate))
+
+    def receive(i):
+        if i:
+            piece = vall.at[source_plane(i), c]
+            push(piece, piece, vz_s.at[i], vz_r.at[i], source_plane(i), c).wait_recv()
+        spread(i, lambda copy: copy.start())
+
+    def forward(i, act, wait):
+        for step in range(1, chips):
+            frm = 2 * lax.rem(chip - step + chips, chips) + core
+            piece = vall.at[source_plane(i), frm]
+            if wait:
+                push(
+                    piece, piece, vb_s.at[i, step - 1], vb_r.at[i, step - 1], d, frm
+                ).wait_recv()
+            act(push(piece, piece, vm_s.at[i, step], vm_r.at[i, step], d, mate))
+
+    def multiply(i):
+        plane = source_plane(i)
+        for step in range(chips):
+            frm = 2 * lax.rem(chip - step + chips, chips) + 1 - core
+            piece = vall.at[plane, frm]
+            push(piece, piece, vm_s.at[i, step], vm_r.at[i, step], d, mate).wait_recv()
+        width = 256
+
+        def tile(index, carry):
+            cols = pl.ds(pl.multiple_of(index * width, width), width)
+            right = vall[plane, :, :, cols].reshape(blocks * tok, width)
+            product = dot(xt[plane], right, 1, 0)
+            wg[:, cols] = product if i == 0 else wg[:, cols] + product
+            return carry
+
+        lax.fori_loop(0, wg.shape[1] // width, tile, 0)
+
+    start = lambda copy: copy.start()
+    done = 1
+    carry_chunk(0)
+    for i in range(planes):
+        if i + 1 < planes:
+            carry_chunk(i + 1)
+        finish(i)
+        if i != 1:
+            receive(max(i - 1, 0))
+        if done < planes - 1 and i % 2 == 0:
+            chain_wait(done)
+            done += 1
+            chain(done, start)
+    forward(0, start, True)
+    receive(planes - 1)
+    while done < planes - 1:
+        chain_wait(done)
+        done += 1
+        chain(done, start)
+    for i in range(1, planes):
+        forward(i, start, True)
+        multiply(i - 1)
+        if i == 1:
+            chain_wait(done)
+    multiply(planes - 1)
+
+    for step in range(1, blocks):
+        through_push(step).wait_send()
+    for step in range(1, planes):
+        chain(step, lambda copy: copy.wait_send())
+    for i in range(planes):
+        mate_push(i).wait_send()
+        carried_push(i).wait_send()
+        for step in range(1, chips):
+            state_push(i, step).wait_send()
+        if i:
+            value_push(i).wait_send()
+        spread(i, lambda copy: copy.wait_send())
+        forward(i, lambda copy: copy.wait_send(), False)
+
+
+def per_device_fused(planes, blocks, inputs, queries, keys, values, out_grad, log_gate, boundaries):
+    tok, feature = queries.shape[1:]
+    heads = log_gate.shape[1]
+    size = feature // heads
+    chunk = heads // planes
+    half = chunk // 2
+    chips = blocks // 2
+    width = feature // planes
+    rows = inputs.shape[2] // blocks
+    vmem = pl.BlockSpec(memory_space=pltpu.VMEM)
+    sem = pltpu.SemaphoreType.DMA
+    scratch = [
+        pltpu.VMEM((heads, tok), F32),
+        pltpu.VMEM((tok, tok), F32),
+        pltpu.VMEM((tok, tok), F32),
+        pltpu.VMEM((tok, tok), F32),
+        pltpu.VMEM((blocks, heads, size), F32),
+        pltpu.VMEM((inputs.shape[2], tok), BF16),
+        pltpu.VMEM((planes, rows, blocks * tok), BF16),
+        pltpu.VMEM((planes, 2, 2, half, size, size), BF16),
+        pltpu.VMEM((planes, 2, half, size, size), BF16),
+        pltpu.VMEM((planes, 2, half, size, size), BF16),
+        pltpu.VMEM((planes, chips - 1, half, size, size), BF16),
+        pltpu.VMEM((planes, 2, 2, half, size, size), BF16),
+        pltpu.VMEM((planes, 2, half, size, size), BF16),
+        pltpu.VMEM((tok, feature), F32),
+        pltpu.VMEM((tok, feature), F32),
+        pltpu.VMEM((tok, feature), F32),
+        pltpu.VMEM((planes, tok, width), BF16),
+        pltpu.VMEM((planes, blocks, tok, width), BF16),
+        sem((blocks - 1,)), sem((blocks - 1,)),
+        sem((blocks - 1,)), sem((blocks - 1,)),
+        sem((2, planes - 1)), sem((2, planes - 1)),
+        sem((planes,)), sem((planes,)),
+        sem((planes, chips - 1)), sem((planes, chips - 1)),
+        sem((planes,)), sem((planes,)),
+        sem((planes,)), sem((planes,)),
+        sem((planes, chips - 1)), sem((planes, chips - 1)),
+        sem((planes, chips)), sem((planes, chips)),
+    ]
+    query_grad, key_grad, weight_grad = pl.pallas_call(
+        functools.partial(fused, planes, blocks),
+        out_shape=(
+            jax.ShapeDtypeStruct((tok, feature), BF16),
+            jax.ShapeDtypeStruct((tok, feature), BF16),
+            jax.ShapeDtypeStruct((rows, width), F32),
+        ),
+        in_specs=[vmem] * 6 + [pl.BlockSpec(memory_space=pltpu.SMEM)],
+        out_specs=(vmem, vmem, vmem),
+        scratch_shapes=scratch,
+        compiler_params=pltpu.CompilerParams(
+            collective_id=0, has_side_effects=True, vmem_limit_bytes=VMEM_LIMIT
+        ),
+    )(queries[0], keys[0], values[0], out_grad[0], inputs[0], log_gate[0], boundaries)
+    return query_grad[None], key_grad[None], weight_grad
+
+
+VMEM_LIMIT = 60 * 2**20
+
+
+def per_device(mesh, inputs, queries, keys, values, out_grad, log_gate, boundaries):
+    planes, blocks = mesh.shape["dp"], mesh.shape["ctx"]
+    arrays = (inputs, queries, keys, values, out_grad, log_gate, boundaries)
+    tok, feature = queries.shape[1:]
+    gathered = 2 * planes * blocks * tok * (feature // planes + inputs.shape[2] // blocks)
+    if gathered + 32 * tok * feature * 2 > VMEM_LIMIT:
+        return per_device_plain(*arrays)
+    return per_device_fused(planes, blocks, *arrays)
+
+
 def solution(mesh):
     in_specs = (
         P("dp", "ctx", None),
@@ -119,5 +560,5 @@
     )
     out_specs = (P("dp", "ctx", None), P("dp", "ctx", None), P("ctx", "dp"))
     return jax.shard_map(
-        per_device, mesh=mesh, in_specs=in_specs, out_specs=out_specs, check_vma=False
-    )
+        functools.partial(per_device, mesh), mesh=mesh, in_specs=in_specs, out_specs=out_specs, check_vma=False
+    )

time: 215 us -> 121 us (0.56)
  Pallas kernels: 0 us -> 116 us
  waiting for transfers between devices: 88.7 us -> 0 us
  matrix products: 31.3 us -> 0 us
  blocking collectives: 28.4 us -> 0 us
  local copies, waits for them, and re-layouts: 24.4 us -> 4.56 us
  other arithmetic: 14 us -> 0 us
  between operations: 14.3 us -> 0.66 us
  starting transfers between devices: 13.3 us -> 0 us
    pallas_call x0 -> x1, Pallas kernels: none -> 116 us  [per_device_fused(): pl.pallas_call(functools.partial(fused, planes, blocks), out_shape=(jax.S...]
    all_to_all x3 -> x0, waiting for transfers between devices: 51.4 us -> none  [the longest x1 26.4 us: per_device(): carried = lax.all_to_all(carried, 'ctx', 0, 0, tiled=True)]
    all_gather x2 -> x0, waiting for transfers between devices: 37.2 us -> none  [the longest x1 37.2 us: per_device(): value_all = lax.all_gather(value_all, 'ctx')]
    dot_general x10 -> x0, matrix products: 31.3 us -> none  [the longest x1 8.15 us: per_device(): lax.dot_general(token_all, value_all, (((0,), (0,)), ((), ())), preferred...]
    all_to_all x1 -> x0, blocking collectives: 28.4 us -> none  [per_device(): value_all = lax.all_to_all(value_grad, 'dp', 1, 0, tiled=True)]
    all_to_all x3 -> x0, starting transfers between devices: 13.3 us -> none  [the longest x1 5.3 us: per_device(): token_all = lax.all_to_all(token_one, 'ctx', 1, 0, tiled=True)]
    unnamed x38 -> x7, local copies, waits for them, and re-layouts: 14.9 us -> 4.56 us
    unnamed x11 -> x0, other arithmetic: 5.1 us -> none
  transfers between devices with their start and end apart: 5 -> 0, of which waited for: 3 -> 0; matrix products, arithmetic and copies ran while one was open for 25% -> 0% of each run, Pallas kernels for 0% -> 0%
where the time goes in v2:
time: 121 us
  Pallas kernels  116 us (96%)
  local copies, waits for them, and re-layouts  4.56 us (4%)
    pallas_call x1, Pallas kernels, per_device_fused(): pl.pallas_call(functools.partial(fused, planes, blocks), out_shape=(jax.S...  116 us
    unnamed x7, local copies, waits for them, and re-layouts  4.56 us

profile of v2, /device:TPU:0, one launch (start us, length us, event | category | flops | bytes accessed | tf_op | source)
XLA Modules:
  0.0 121.2 jit_solution(15361313228617337689)
XLA Ops:
  0.6 116.0 %shard_map.94 = (bf16[128,4096]{1,0:T(8,128)(2,1)}, bf16[128,4096]{1,0:T(8,128)(2,1)}, f32[384,1024]{1,0:T(8,128)}) custom-call(bf16[128,4096]{1,0:T(8,128)(2,1)} %bitcast.8, bf16[128,4096]{1,0:T(8,128)(2,1)} %bitcast.9, bf16[128,4096]{1,0:T(8,128)(2,1)} %bitcast.10, bf16[128,4096]{1,0:T(8,128)(2,1)} %bitcast.11, bf16[128,3072]{1,0:T(8,128)(2,1)} %bitcast.14, ...), custom_call_target="tpu_custom_call" | custom-call | tf_op jit(solution)/shard_map/pallas_call | solution.py:521
  116.6 0.0 copy-start.1
  116.6 0.0 copy-start
  116.6 2.4 %copy.13 = bf16[1,128,4096]{2,1,0:T(8,128)(2,1)} copy(bf16[1,128,4096]{2,1,0:T(8,128)(2,1)} %bitcast.13) | data formatting | bytes 2097152
  119.1 0.0 copy-done.1
  119.1 1.0 copy.14
  120.0 0.0 copy-done
  120.0 1.1 copy.15
Async XLA Ops:
  116.6 2.5 %copy-start.1 = (bf16[128,4096]{1,0:T(8,128)(2,1)S(1)}, bf16[128,4096]{1,0:T(8,128)(2,1)}, u32[]{:S(2)}) copy-start(bf16[128,4096]{1,0:T(8,128)(2,1)} %get-tuple-element.7) | copy-start | bytes 3145732
  116.6 3.4 %copy-start = (f32[384,1024]{1,0:T(8,128)S(1)}, f32[384,1024]{1,0:T(8,128)}, u32[]{:S(2)}) copy-start(f32[384,1024]{1,0:T(8,128)} %get-tuple-element.14) | copy-start | bytes 4718596

commit v3 on v2

--- a/solution.py
+++ b/solution.py
@@ -228,25 +228,29 @@
     def mate_push(i):
         return push(local.at[i, 1 - core], mate_local.at[i], m1_s.at[i], m1_r.at[i], d, mate)
 
-    def local_chunk(i, carry):
-        for j in range(chunk):
-            head = chunk_head(i, j)
-            cols = head_columns(head)
-            _, _, enter, leave = weights(head)
-            weighted_keys = (leave * k[:, cols].astype(F32)).astype(BF16)
-            weighted_queries = (enter * q[:, cols].astype(F32)).astype(BF16)
-            local[i, j // half, 0, j % half] = dot(weighted_keys, v[:, cols], 0, 0).astype(BF16)
-            local[i, j // half, 1, j % half] = dot(weighted_queries, g[:, cols], 0, 0).astype(BF16)
+    def halves(body):
+        lax.fori_loop(0, 2, lambda part, carry: (body(part), carry)[1], 0)
+
+    def local_chunk(i):
+        def body(part):
+            for j in range(half):
+                head = chunk_head(i, part * half + j)
+                cols = head_columns(head)
+                _, _, enter, leave = weights(head)
+                weighted_keys = (leave * k[:, cols].astype(F32)).astype(BF16)
+                weighted_queries = (enter * q[:, cols].astype(F32)).astype(BF16)
+                local[i, part, 0, j] = dot(weighted_keys, v[:, cols], 0, 0).astype(BF16)
+                local[i, part, 1, j] = dot(weighted_queries, g[:, cols], 0, 0).astype(BF16)
+
+        halves(body)
         mate_push(i).start()
-        return carry
-
-    lax.fori_loop(0, planes, local_chunk, 0)
-
-    for step in range(1, blocks):
-        frm = lax.rem(c - step + blocks, blocks)
-        push(
-            through.at[frm], through.at[frm], t_s.at[step - 1], t_r.at[step - 1], d, frm
-        ).wait_recv()
+
+    def through_wait():
+        for step in range(1, blocks):
+            frm = lax.rem(c - step + blocks, blocks)
+            push(
+                through.at[frm], through.at[frm], t_s.at[step - 1], t_r.at[step - 1], d, frm
+            ).wait_recv()
 
     def state_push(i, step):
         ahead = chip + step
@@ -255,7 +259,7 @@
             cs_s.at[i, step - 1], cs_r.at[i, step - 1], d, 2 * lax.rem(ahead, chips) + core,
         )
 
-    def chip_chunk(i, carry):
+    def chip_chunk(i):
         mate_push(i).wait_recv()
         for j in range(half):
             head = chunk_head(i, core * half + j)
@@ -271,17 +275,15 @@
             ).astype(BF16)
         for step in range(1, chips):
             state_push(i, step).start()
-        return carry
-
-    lax.fori_loop(0, planes, chip_chunk, 0)
-
-    for step in range(1, blocks):
-        token_push(step).wait_send()
-        frm = lax.rem(c - step + blocks, blocks)
-        push(
-            xt.at[d, :, columns(frm)], xt.at[d, :, columns(frm)],
-            xa_s.at[step - 1], xa_r.at[step - 1], d, frm,
-        ).wait_recv()
+
+    def token_wait():
+        for step in range(1, blocks):
+            token_push(step).wait_send()
+            frm = lax.rem(c - step + blocks, blocks)
+            push(
+                xt.at[d, :, columns(frm)], xt.at[d, :, columns(frm)],
+                xa_s.at[step - 1], xa_r.at[step - 1], d, frm,
+            ).wait_recv()
 
     def chain(step, act):
         @pl.when((d >= step - 1) & (d + 1 < planes))
@@ -305,25 +307,21 @@
             piece = xt.at[d + step]
             push(piece, piece, xz_s.at[1, step - 1], xz_r.at[1, step - 1], d + 1, c).wait_recv()
 
-    chain(1, lambda copy: copy.start())
-
-    group = 4
-
-    def inner(index, carry):
-        for j in range(group):
-            head = index * group + j
-            cols = head_columns(head)
-            at_row = jnp.broadcast_to(cum[pl.ds(head, 1), :], (size, tok))
-            decay = jnp.exp(at_row.T - at_row + decay_bias[...])
-            qh, kh, vh, gh = q[:, cols], k[:, cols], v[:, cols], g[:, cols]
-            score_grad = (decay * dot(gh, vh, 1, 1)).astype(BF16)
-            score_keys = (decay * dot(qh, kh, 1, 1)).astype(BF16)
-            qi[:, cols] = dot(score_grad, kh, 1, 0)
-            ki[:, cols] = dot(score_grad, qh, 0, 0)
-            vi[:, cols] = dot(score_keys, gh, 0, 0)
-        return carry
-
-    lax.fori_loop(0, heads // group, inner, 0)
+    def inner_chunk(i):
+        def body(part):
+            for j in range(half):
+                head = chunk_head(i, part * half + j)
+                cols = head_columns(head)
+                at_row = jnp.broadcast_to(cum[pl.ds(head, 1), :], (size, tok))
+                decay = jnp.exp(at_row.T - at_row + decay_bias[...])
+                qh, kh, vh, gh = q[:, cols], k[:, cols], v[:, cols], g[:, cols]
+                score_grad = (decay * dot(gh, vh, 1, 1)).astype(BF16)
+                score_keys = (decay * dot(qh, kh, 1, 1)).astype(BF16)
+                qi[:, cols] = dot(score_grad, kh, 1, 0)
+                ki[:, cols] = dot(score_grad, qh, 0, 0)
+                vi[:, cols] = dot(score_keys, gh, 0, 0)
+
+        halves(body)
 
     def carried_push(i):
         return push(mate_carried.at[i], carried.at[i, core], m2_s.at[i], m2_r.at[i], d, mate)
@@ -378,17 +376,19 @@
         push(
             carried.at[i, 1 - core], carried.at[i, 1 - core], m2_s.at[i], m2_r.at[i], d, mate
         ).wait_recv()
-        for j in range(chunk):
-            head = chunk_head(i, j)
-            cols = head_columns(head)
-            _, _, enter, leave = weights(head)
-            came = carried[i, j // half, 0, j % half]
-            back = carried[i, j // half, 1, j % half]
-            vsend[i, :, j * size : (j + 1) * size] = (
-                vi[:, cols] + leave * dot(k[:, cols], back, 1, 0)
-            ).astype(BF16)
-            qg[:, cols] = (qi[:, cols] + enter * dot(g[:, cols], came, 1, 1)).astype(BF16)
-            kg[:, cols] = (ki[:, cols] + leave * dot(v[:, cols], back, 1, 1)).astype(BF16)
+        def body(part):
+            for j in range(half):
+                head = chunk_head(i, part * half + j)
+                cols = head_columns(head)
+                _, _, enter, leave = weights(head)
+                came, back = carried[i, part, 0, j], carried[i, part, 1, j]
+                vsend[i, :, head_columns(part * half + j)] = (
+                    vi[:, cols] + leave * dot(k[:, cols], back, 1, 0)
+                ).astype(BF16)
+                qg[:, cols] = (qi[:, cols] + enter * dot(g[:, cols], came, 1, 1)).astype(BF16)
+                kg[:, cols] = (ki[:, cols] + leave * dot(v[:, cols], back, 1, 1)).astype(BF16)
+
+        halves(body)
         if i == 0:
             vall[d, c] = vsend[0]
         else:
@@ -438,30 +438,47 @@
         lax.fori_loop(0, wg.shape[1] // width, tile, 0)
 
     start = lambda copy: copy.start()
+    last = planes - 1
+
+    local_chunk(0)
+    for i in range(1, planes + 1):
+        if i < planes:
+            local_chunk(i)
+        if i == 1:
+            through_wait()
+        chip_chunk(i - 1)
+        if i == min(2, planes):
+            token_wait()
+            chain(1, start)
+    inner_chunk(0)
+    carry_chunk(0)
     done = 1
-    carry_chunk(0)
     for i in range(planes):
-        if i + 1 < planes:
-            carry_chunk(i + 1)
+        if i < last:
+            inner_chunk(i + 1)
         finish(i)
-        if i != 1:
-            receive(max(i - 1, 0))
-        if done < planes - 1 and i % 2 == 0:
+        if i == 0:
+            receive(0)
+        elif i > 1:
+            receive(i - 1)
+            forward(i - 2, start, True)
+        if done < last and i in (0, 2):
             chain_wait(done)
             done += 1
             chain(done, start)
-    forward(0, start, True)
-    receive(planes - 1)
-    while done < planes - 1:
+        if i < last:
+            carry_chunk(i + 1)
+    while done < last:
         chain_wait(done)
         done += 1
         chain(done, start)
+    receive(last)
+    forward(last - 1, start, True)
+    multiply(0)
+    forward(last, start, True)
+    chain_wait(done)
     for i in range(1, planes):
-        forward(i, start, True)
-        multiply(i - 1)
-        if i == 1:
-            chain_wait(done)
-    multiply(planes - 1)
+        multiply(i)
 
     for step in range(1, blocks):
         through_push(step).wait_send()

time: 121 us -> 123 us (1.017)
  Pallas kernels: 116 us -> 118 us
    pallas_call x1, Pallas kernels: 116 us -> 118 us  [per_device_fused(): pl.pallas_call(functools.partial(fused, planes, blocks), out_shape=(jax.S...]
where the time goes in v3:
time: 123 us
  Pallas kernels  118 us (96%)
  local copies, waits for them, and re-layouts  4.56 us (4%)
    pallas_call x1, Pallas kernels, per_device_fused(): pl.pallas_call(functools.partial(fused, planes, blocks), out_shape=(jax.S...  118 us
    unnamed x7, local copies, waits for them, and re-layouts  4.56 us

profile of v3, /device:TPU:0, one launch (start us, length us, event | category | flops | bytes accessed | tf_op | source)
XLA Modules:
  0.0 123.3 jit_solution(14127709157801574305)
XLA Ops:
  0.6 118.1 %shard_map.94 = (bf16[128,4096]{1,0:T(8,128)(2,1)}, bf16[128,4096]{1,0:T(8,128)(2,1)}, f32[384,1024]{1,0:T(8,128)}) custom-call(bf16[128,4096]{1,0:T(8,128)(2,1)} %bitcast.8, bf16[128,4096]{1,0:T(8,128)(2,1)} %bitcast.9, bf16[128,4096]{1,0:T(8,128)(2,1)} %bitcast.10, bf16[128,4096]{1,0:T(8,128)(2,1)} %bitcast.11, bf16[128,3072]{1,0:T(8,128)(2,1)} %bitcast.14, ...), custom_call_target="tpu_custom_call" | custom-call | tf_op jit(solution)/shard_map/pallas_call | solution.py:538
  118.7 0.0 copy-start.1
  118.8 0.0 copy-start
  118.8 2.4 %copy.13 = bf16[1,128,4096]{2,1,0:T(8,128)(2,1)} copy(bf16[1,128,4096]{2,1,0:T(8,128)(2,1)} %bitcast.13) | data formatting | bytes 2097152
  121.2 0.0 copy-done.1
  121.2 1.0 copy.14
  122.2 0.0 copy-done
  122.2 1.1 copy.15
Async XLA Ops:
  118.7 2.5 %copy-start.1 = (bf16[128,4096]{1,0:T(8,128)(2,1)S(1)}, bf16[128,4096]{1,0:T(8,128)(2,1)}, u32[]{:S(2)}) copy-start(bf16[128,4096]{1,0:T(8,128)(2,1)} %get-tuple-element.7) | copy-start | bytes 3145732
  118.8 3.4 %copy-start = (f32[384,1024]{1,0:T(8,128)S(1)}, f32[384,1024]{1,0:T(8,128)}, u32[]{:S(2)}) copy-start(f32[384,1024]{1,0:T(8,128)} %get-tuple-element.14) | copy-start | bytes 4718596

commit v4 on v3

--- a/solution.py
+++ b/solution.py
@@ -397,11 +397,14 @@
     def source_plane(i):
         return lax.rem(d - i + planes, planes)
 
+    across = chip + 1 - 2 * lax.rem(chip, 2)
+    along = lax.rem(chip + 2, chips)
+    corner = chips - 1 - chip
+
     def spread(i, act):
         piece = vall.at[source_plane(i), c]
-        for step in range(1, chips):
-            to = 2 * lax.rem(chip + step, chips) + core
-            act(push(piece, piece, vb_s.at[i, step - 1], vb_r.at[i, step - 1], d, to))
+        for slot, to in enumerate((across, along)):
+            act(push(piece, piece, vb_s.at[i, slot], vb_r.at[i, slot], d, 2 * to + core))
         act(push(piece, piece, vm_s.at[i, 0], vm_r.at[i, 0], d, mate))
 
     def receive(i):
@@ -411,21 +414,32 @@
         spread(i, lambda copy: copy.start())
 
     def forward(i, act, wait):
-        for step in range(1, chips):
-            frm = 2 * lax.rem(chip - step + chips, chips) + core
-            piece = vall.at[source_plane(i), frm]
+        for slot, (frm, to) in enumerate(((across, along), (along, across))):
+            piece = vall.at[source_plane(i), 2 * frm + core]
             if wait:
                 push(
-                    piece, piece, vb_s.at[i, step - 1], vb_r.at[i, step - 1], d, frm
+                    piece, piece, vb_s.at[i, slot], vb_r.at[i, slot], d, 2 * frm + core
                 ).wait_recv()
-            act(push(piece, piece, vm_s.at[i, step], vm_r.at[i, step], d, mate))
+            part = vall.at[source_plane(i), 2 * frm + core, pl.ds(slot * (tok // 2), tok // 2), :]
+            act(push(part, part, vb_s.at[i, 2 + slot], vb_r.at[i, 2 + slot], d, 2 * to + core))
+            act(push(piece, piece, vm_s.at[i, 1 + slot], vm_r.at[i, 1 + slot], d, mate))
+
+    def forward_corner(i, act, wait):
+        frm = 2 * corner + core
+        if wait:
+            for slot, via in enumerate((along, across)):
+                part = vall.at[source_plane(i), frm, pl.ds(slot * (tok // 2), tok // 2), :]
+                push(
+                    part, part, vb_s.at[i, 2 + slot], vb_r.at[i, 2 + slot], d, 2 * via + core
+                ).wait_recv()
+        piece = vall.at[source_plane(i), frm]
+        act(push(piece, piece, vm_s.at[i, 3], vm_r.at[i, 3], d, mate))
 
     def multiply(i):
         plane = source_plane(i)
-        for step in range(chips):
-            frm = 2 * lax.rem(chip - step + chips, chips) + 1 - core
-            piece = vall.at[plane, frm]
-            push(piece, piece, vm_s.at[i, step], vm_r.at[i, step], d, mate).wait_recv()
+        for slot, frm in enumerate((chip, across, along, corner)):
+            piece = vall.at[plane, 2 * frm + 1 - core]
+            push(piece, piece, vm_s.at[i, slot], vm_r.at[i, slot], d, mate).wait_recv()
         width = 256
 
         def tile(index, carry):
@@ -452,31 +466,37 @@
             chain(1, start)
     inner_chunk(0)
     carry_chunk(0)
-    done = 1
     for i in range(planes):
         if i < last:
             inner_chunk(i + 1)
+        if i == 0:
+            chain_wait(1)
+            chain(2, start)
         finish(i)
         if i == 0:
             receive(0)
-        elif i > 1:
+        elif i == 1:
+            forward(0, start, True)
+        else:
+            if i == last:
+                for step in range(2, last):
+                    chain_wait(step)
+                    chain(step + 1, start)
             receive(i - 1)
-            forward(i - 2, start, True)
-        if done < last and i in (0, 2):
-            chain_wait(done)
-            done += 1
-            chain(done, start)
+            if i == 2:
+                forward_corner(0, start, True)
+            else:
+                forward(i - 2, start, True)
         if i < last:
             carry_chunk(i + 1)
-    while done < last:
-        chain_wait(done)
-        done += 1
-        chain(done, start)
     receive(last)
     forward(last - 1, start, True)
+    for i in range(1, last):
+        forward_corner(i, start, True)
     multiply(0)
     forward(last, start, True)
-    chain_wait(done)
+    forward_corner(last, start, True)
+    chain_wait(last)
     for i in range(1, planes):
         multiply(i)
 
@@ -493,6 +513,7 @@
             value_push(i).wait_send()
         spread(i, lambda copy: copy.wait_send())
         forward(i, lambda copy: copy.wait_send(), False)
+        forward_corner(i, lambda copy: copy.wait_send(), False)
 
 
 def per_device_fused(planes, blocks, inputs, queries, keys, values, out_grad, log_gate, boundaries):
@@ -532,7 +553,7 @@
         sem((planes, chips - 1)), sem((planes, chips - 1)),
         sem((planes,)), sem((planes,)),
         sem((planes,)), sem((planes,)),
-        sem((planes, chips - 1)), sem((planes, chips - 1)),
+        sem((planes, chips)), sem((planes, chips)),
         sem((planes, chips)), sem((planes, chips)),
     ]
     query_grad, key_grad, weight_grad = pl.pallas_call(
@@ -560,7 +581,7 @@
     arrays = (inputs, queries, keys, values, out_grad, log_gate, boundaries)
     tok, feature = queries.shape[1:]
     gathered = 2 * planes * blocks * tok * (feature // planes + inputs.shape[2] // blocks)
-    if gathered + 32 * tok * feature * 2 > VMEM_LIMIT:
+    if blocks != 8 or planes < 3 or gathered + 32 * tok * feature * 2 > VMEM_LIMIT:
         return per_device_plain(*arrays)
     return per_device_fused(planes, blocks, *arrays)
 

time: 123 us -> 115 us (0.935)
  the two profiles are of different devices: /device:TPU:0 before, /device:TPU:16 now
where the time goes in v4:
time: 115 us
  Pallas kernels  109 us (95%)
  local copies, waits for them, and re-layouts  4.56 us (4%)
    pallas_call x1, Pallas kernels, per_device_fused(): pl.pallas_call(functools.partial(fused, planes, blocks), out_shape=(jax.S...  109 us
    unnamed x7, local copies, waits for them, and re-layouts  4.56 us

profile of v4, /device:TPU:16, one launch (start us, length us, event | category | flops | bytes accessed | tf_op | source)
XLA Modules:
  0.0 114.6 jit_solution(7337377926345081494)
XLA Ops:
  0.6 109.4 %shard_map.94 = (bf16[128,4096]{1,0:T(8,128)(2,1)}, bf16[128,4096]{1,0:T(8,128)(2,1)}, f32[384,1024]{1,0:T(8,128)}) custom-call(bf16[128,4096]{1,0:T(8,128)(2,1)} %bitcast.8, bf16[128,4096]{1,0:T(8,128)(2,1)} %bitcast.9, bf16[128,4096]{1,0:T(8,128)(2,1)} %bitcast.10, bf16[128,4096]{1,0:T(8,128)(2,1)} %bitcast.11, bf16[128,3072]{1,0:T(8,128)(2,1)} %bitcast.14, ...), custom_call_target="tpu_custom_call" | custom-call | tf_op jit(solution)/shard_map/pallas_call | solution.py:559
  110.0 0.0 copy-start.1
  110.0 0.0 copy-start
  110.0 2.4 %copy.13 = bf16[1,128,4096]{2,1,0:T(8,128)(2,1)} copy(bf16[1,128,4096]{2,1,0:T(8,128)(2,1)} %bitcast.13) | data formatting | bytes 2097152
  112.5 0.0 copy-done.1
  112.5 1.0 copy.14
  113.4 0.0 copy-done
  113.4 1.1 copy.15
Async XLA Ops:
  110.0 2.5 %copy-start.1 = (bf16[128,4096]{1,0:T(8,128)(2,1)S(1)}, bf16[128,4096]{1,0:T(8,128)(2,1)}, u32[]{:S(2)}) copy-start(bf16[128,4096]{1,0:T(8,128)(2,1)} %get-tuple-element.7) | copy-start | bytes 3145732
  110.0 3.4 %copy-start = (f32[384,1024]{1,0:T(8,128)S(1)}, f32[384,1024]{1,0:T(8,128)}, u32[]{:S(2)}) copy-start(f32[384,1024]{1,0:T(8,128)} %get-tuple-element.14) | copy-start | bytes 4718596

commit v5 on v4

--- a/solution.py
+++ b/solution.py
@@ -223,7 +223,7 @@
         return at_row, at_col, enter, leave
 
     def chunk_head(i, j):
-        return lax.rem(d + i, planes) * chunk + j
+        return lax.rem(d + i + 1, planes) * chunk + j
 
     def mate_push(i):
         return push(local.at[i, 1 - core], mate_local.at[i], m1_s.at[i], m1_r.at[i], d, mate)
@@ -369,7 +369,7 @@
 
     def value_push(i):
         return push(
-            vsend.at[i], vall.at[d, c], vz_s.at[i], vz_r.at[i], lax.rem(d + i, planes), c
+            vsend.at[i], vall.at[d, c], vz_s.at[i], vz_r.at[i], lax.rem(d + i + 1, planes), c
         )
 
     def finish(i):
@@ -389,13 +389,13 @@
                 kg[:, cols] = (ki[:, cols] + leave * dot(v[:, cols], back, 1, 1)).astype(BF16)
 
         halves(body)
-        if i == 0:
-            vall[d, c] = vsend[0]
+        if i == planes - 1:
+            vall[d, c] = vsend[i]
         else:
             value_push(i).start()
 
     def source_plane(i):
-        return lax.rem(d - i + planes, planes)
+        return lax.rem(d - i - 1 + planes, planes)
 
     across = chip + 1 - 2 * lax.rem(chip, 2)
     along = lax.rem(chip + 2, chips)
@@ -408,7 +408,7 @@
         act(push(piece, piece, vm_s.at[i, 0], vm_r.at[i, 0], d, mate))
 
     def receive(i):
-        if i:
+        if i < planes - 1:
             piece = vall.at[source_plane(i), c]
             push(piece, piece, vz_s.at[i], vz_r.at[i], source_plane(i), c).wait_recv()
         spread(i, lambda copy: copy.start())
@@ -473,31 +473,25 @@
             chain_wait(1)
             chain(2, start)
         finish(i)
-        if i == 0:
-            receive(0)
-        elif i == 1:
-            forward(0, start, True)
-        else:
-            if i == last:
-                for step in range(2, last):
-                    chain_wait(step)
-                    chain(step + 1, start)
+        if i == last - 1:
+            for step in range(2, last):
+                chain_wait(step)
+                chain(step + 1, start)
+        if i == last:
+            receive(last)
+        if i > 0:
             receive(i - 1)
-            if i == 2:
-                forward_corner(0, start, True)
-            else:
-                forward(i - 2, start, True)
+        if i > 1:
+            forward(i - 2, start, True)
         if i < last:
             carry_chunk(i + 1)
-    receive(last)
+    forward_corner(0, start, True)
     forward(last - 1, start, True)
-    for i in range(1, last):
+    forward(last, start, True)
+    for i in range(1, planes):
         forward_corner(i, start, True)
-    multiply(0)
-    forward(last, start, True)
-    forward_corner(last, start, True)
     chain_wait(last)
-    for i in range(1, planes):
+    for i in range(planes):
         multiply(i)
 
     for step in range(1, blocks):
@@ -509,7 +503,7 @@
         carried_push(i).wait_send()
         for step in range(1, chips):
             state_push(i, step).wait_send()
-        if i:
+        if i < last:
             value_push(i).wait_send()
         spread(i, lambda copy: copy.wait_send())
         forward(i, lambda copy: copy.wait_send(), False)

time: 115 us -> 122 us (1.061)
  the two profiles are of different devices: /device:TPU:16 before, /device:TPU:0 now
where the time goes in v5:
time: 122 us; the launch traced here: 119 us
  Pallas kernels  114 us (93%)
  local copies, waits for them, and re-layouts  4.56 us (4%)
    pallas_call x1, Pallas kernels, per_device_fused(): pl.pallas_call(functools.partial(fused, planes, blocks), out_shape=(jax.S...  114 us
    unnamed x7, local copies, waits for them, and re-layouts  4.56 us

profile of v5, /device:TPU:0, one launch (start us, length us, event | category | flops | bytes accessed | tf_op | source)
XLA Modules:
  0.0 119.3 jit_solution(16283945578664010078)
XLA Ops:
  0.6 114.0 %shard_map.94 = (bf16[128,4096]{1,0:T(8,128)(2,1)}, bf16[128,4096]{1,0:T(8,128)(2,1)}, f32[384,1024]{1,0:T(8,128)}) custom-call(bf16[128,4096]{1,0:T(8,128)(2,1)} %bitcast.8, bf16[128,4096]{1,0:T(8,128)(2,1)} %bitcast.9, bf16[128,4096]{1,0:T(8,128)(2,1)} %bitcast.10, bf16[128,4096]{1,0:T(8,128)(2,1)} %bitcast.11, bf16[128,3072]{1,0:T(8,128)(2,1)} %bitcast.14, ...), custom_call_target="tpu_custom_call" | custom-call | tf_op jit(solution)/shard_map/pallas_call | solution.py:553
  114.7 0.0 copy-start.1
  114.7 0.0 copy-start
  114.7 2.4 %copy.13 = bf16[1,128,4096]{2,1,0:T(8,128)(2,1)} copy(bf16[1,128,4096]{2,1,0:T(8,128)(2,1)} %bitcast.13) | data formatting | bytes 2097152
  117.1 0.0 copy-done.1
  117.1 1.0 copy.14
  118.1 0.0 copy-done
  118.1 1.1 copy.15
Async XLA Ops:
  114.7 2.5 %copy-start.1 = (bf16[128,4096]{1,0:T(8,128)(2,1)S(1)}, bf16[128,4096]{1,0:T(8,128)(2,1)}, u32[]{:S(2)}) copy-start(bf16[128,4096]{1,0:T(8,128)(2,1)} %get-tuple-element.7) | copy-start | bytes 3145732
  114.7 3.4 %copy-start = (f32[384,1024]{1,0:T(8,128)S(1)}, f32[384,1024]{1,0:T(8,128)}, u32[]{:S(2)}) copy-start(f32[384,1024]{1,0:T(8,128)} %get-tuple-element.14) | copy-start | bytes 4718596

commit v6 on v4

--- a/solution.py
+++ b/solution.py
@@ -132,7 +132,8 @@
 
 
 def fused(
-    planes, blocks, q, k, v, g, x, gate, bounds, qg, kg, wg,
+    planes, blocks, q_in, k_in, v_in, g_in, x_in, gate, bounds, qg_out, kg_out, wg,
+    q, k, v, g, x, qg, kg, acc, io_sem,
     cum, decay_bias, enter_bias, leave_bias, through, xt_own, xt,
     local, mate_local, chip_state, arrived, carried, mate_carried, qi, ki, vi, vsend, vall,
     t_s, t_r, xa_s, xa_r, xz_s, xz_r, m1_s, m1_r, cs_s, cs_r, m2_s, m2_r, vz_s, vz_r,
@@ -162,6 +163,15 @@
             device_id_type=pl.DeviceIdType.MESH,
         )
 
+    loads = [
+        pltpu.make_async_copy(src, dst, io_sem.at[index])
+        for index, (src, dst) in enumerate(
+            ((x_in, x), (k_in, k), (q_in, q), (v_in, v), (g_in, g))
+        )
+    ]
+    for load in loads:
+        load.start()
+    loads[0].wait()
     for part in range(x.shape[1] // 128):
         xt_own[part * 128 : (part + 1) * 128, :] = x[:, part * 128 : (part + 1) * 128].T
     pl.semaphore_wait(barrier, blocks - 1 + planes - 1)
@@ -446,13 +456,21 @@
             cols = pl.ds(pl.multiple_of(index * width, width), width)
             right = vall[plane, :, :, cols].reshape(blocks * tok, width)
             product = dot(xt[plane], right, 1, 0)
-            wg[:, cols] = product if i == 0 else wg[:, cols] + product
+            if i:
+                product = acc[:, cols] + product
+            if i == planes - 1:
+                wg[:, cols] = product.astype(BF16)
+            else:
+                acc[:, cols] = product
             return carry
 
-        lax.fori_loop(0, wg.shape[1] // width, tile, 0)
+        lax.fori_loop(0, acc.shape[1] // width, tile, 0)
 
     start = lambda copy: copy.start()
     last = planes - 1
+
+    for load in loads[1:]:
+        load.wait()
 
     local_chunk(0)
     for i in range(1, planes + 1):
@@ -489,16 +507,26 @@
                 forward(i - 2, start, True)
         if i < last:
             carry_chunk(i + 1)
+    stores = [
+        pltpu.make_async_copy(src, dst, io_sem.at[5 + index])
+        for index, (src, dst) in enumerate(((qg, qg_out), (kg, kg_out)))
+    ]
+    for store in stores:
+        store.start()
     receive(last)
     forward(last - 1, start, True)
     for i in range(1, last):
         forward_corner(i, start, True)
     multiply(0)
     forward(last, start, True)
+    for i in range(2, last):
+        multiply(i)
     forward_corner(last, start, True)
     chain_wait(last)
-    for i in range(1, planes):
-        multiply(i)
+    multiply(1)
+    multiply(last)
+    for store in stores:
+        store.wait()
 
     for step in range(1, blocks):
         through_push(step).wait_send()
@@ -526,8 +554,18 @@
     width = feature // planes
     rows = inputs.shape[2] // blocks
     vmem = pl.BlockSpec(memory_space=pltpu.VMEM)
+    hbm = pl.BlockSpec(memory_space=pl.ANY)
     sem = pltpu.SemaphoreType.DMA
     scratch = [
+        pltpu.VMEM((tok, feature), BF16),
+        pltpu.VMEM((tok, feature), BF16),
+        pltpu.VMEM((tok, feature), BF16),
+        pltpu.VMEM((tok, feature), BF16),
+        pltpu.VMEM((tok, inputs.shape[2]), BF16),
+        pltpu.VMEM((tok, feature), BF16),
+        pltpu.VMEM((tok, feature), BF16),
+        pltpu.VMEM((rows, width), F32),
+        sem((7,)),
         pltpu.VMEM((heads, tok), F32),
         pltpu.VMEM((tok, tok), F32),
         pltpu.VMEM((tok, tok), F32),
@@ -561,16 +599,16 @@
         out_shape=(
             jax.ShapeDtypeStruct((tok, feature), BF16),
             jax.ShapeDtypeStruct((tok, feature), BF16),
-            jax.ShapeDtypeStruct((rows, width), F32),
+            jax.ShapeDtypeStruct((rows, width), BF16),
         ),
-        in_specs=[vmem] * 6 + [pl.BlockSpec(memory_space=pltpu.SMEM)],
-        out_specs=(vmem, vmem, vmem),
+        in_specs=[hbm] * 5 + [vmem] + [pl.BlockSpec(memory_space=pltpu.SMEM)],
+        out_specs=(hbm, hbm, vmem),
         scratch_shapes=scratch,
         compiler_params=pltpu.CompilerParams(
             collective_id=0, has_side_effects=True, vmem_limit_bytes=VMEM_LIMIT
         ),
     )(queries[0], keys[0], values[0], out_grad[0], inputs[0], log_gate[0], boundaries)
-    return query_grad[None], key_grad[None], weight_grad
+    return query_grad[None], key_grad[None], weight_grad.astype(F32)
 
 
 VMEM_LIMIT = 60 * 2**20
@@ -581,7 +619,7 @@
     arrays = (inputs, queries, keys, values, out_grad, log_gate, boundaries)
     tok, feature = queries.shape[1:]
     gathered = 2 * planes * blocks * tok * (feature // planes + inputs.shape[2] // blocks)
-    if blocks != 8 or planes < 3 or gathered + 32 * tok * feature * 2 > VMEM_LIMIT:
+    if blocks != 8 or planes < 4 or gathered + 32 * tok * feature * 2 > VMEM_LIMIT:
         return per_device_plain(*arrays)
     return per_device_fused(planes, blocks, *arrays)
 

time: 115 us -> 112 us (0.974)
  the two profiles are of different devices: /device:TPU:16 before, /device:TPU:17 now
where the time goes in v6:
time: 112 us; the launch traced here: 111 us
  Pallas kernels  106 us (95%)
  local copies, waits for them, and re-layouts  2.58 us (2%)
  other arithmetic  2.54 us (2%)
    pallas_call x1, Pallas kernels, per_device_fused(): pl.pallas_call(functools.partial(fused, planes, blocks), out_shape=(jax.S...  106 us
    unnamed x6, local copies, waits for them, and re-layouts  2.58 us
    convert_element_type x1, other arithmetic, per_device_fused(): return (query_grad[None], key_grad[None], weight_grad.astype(F32))  2.54 us

profile of v6, /device:TPU:17, one launch (start us, length us, event | category | flops | bytes accessed | tf_op | source)
XLA Modules:
  0.0 111.3 jit_solution(12380773218995944390)
XLA Ops:
  0.6 105.5 %shard_map.94 = (bf16[128,4096]{1,0:T(8,128)(2,1)}, bf16[128,4096]{1,0:T(8,128)(2,1)}, bf16[384,1024]{1,0:T(8,128)(2,1)}) custom-call(bf16[128,4096]{1,0:T(8,128)(2,1)} %bitcast.8, bf16[128,4096]{1,0:T(8,128)(2,1)} %bitcast.9, bf16[128,4096]{1,0:T(8,128)(2,1)} %bitcast.10, bf16[128,4096]{1,0:T(8,128)(2,1)} %bitcast.11, bf16[128,3072]{1,0:T(8,128)(2,1)} %bitcast.14, ...), custom_call_target="tpu_custom_call" | custom-call | tf_op jit(solution)/shard_map/pallas_call | solution.py:597
  106.1 0.0 copy-start.1
  106.2 2.5 %convert_element_type.3 = f32[384,1024]{1,0:T(8,128)} convert(bf16[384,1024]{1,0:T(8,128)(2,1)} %get-tuple-element.8) | non-fusion elementwise | flops 393216 | bytes 2359296 | tf_op jit(solution)/shard_map/convert_element_type | solution.py:611
  108.7 0.0 copy-done.1
  108.7 0.0 copy-start
  108.7 1.0 copy.12
  109.7 0.6 copy-done
  110.3 1.0 copy.13
Async XLA Ops:
  106.1 2.6 %copy-start.1 = (bf16[128,4096]{1,0:T(8,128)(2,1)S(1)}, bf16[128,4096]{1,0:T(8,128)(2,1)}, u32[]{:S(2)}) copy-start(bf16[128,4096]{1,0:T(8,128)(2,1)} %get-tuple-element.6) | copy-start | bytes 3145732
  108.7 1.6 %copy-start = (bf16[128,4096]{1,0:T(8,128)(2,1)S(1)}, bf16[128,4096]{1,0:T(8,128)(2,1)}, u32[]{:S(2)}) copy-start(bf16[128,4096]{1,0:T(8,128)(2,1)} %get-tuple-element.7) | copy-start | bytes 3145732
